TPU v7x, 128 devices: a whole 4x4x4 slice. The times are simulated.
128 devices in a mesh: dp: 16 (over y, z_lo, core), section: 4 (over x), grp: 2 (over z_hi).
Axes of the slice: x: 4, y: 4, z: 4 (z_hi: 2, z_lo: 2; z = z_hi * 2 + z_lo), core: 2. Of those that a mesh axis runs over, the one named last changes fastest.
Arguments:
- enc_input: bfloat16 [2, 64, 48, 4096], P(None, ('dp', 'section')), may hold values from -20 to 20
- weights: bfloat16 [2, 4096, 1024], P('grp'), may hold values from -0.75 to 0.75
- enc_gain: float32 [4096], replicated, may hold values from 0.1 to 1.9
- enc_bias: float32 [1024], replicated, may hold values from -3 to 3
- mask_token: float32 [1024], replicated, may hold values from -6 to 6
- pos_embed: float32 [192, 1024], replicated, may hold values from -6 to 6
- dec_gains: float32 [2, 1024], replicated, may hold values from 0.1 to 1.9
- head_weight: bfloat16 [1024, 256], replicated, may hold values from -0.1875 to 0.1875
- head_bias: float32 [256], replicated, may hold values from -3 to 3
- order: int32 [2, 64, 192], P(None, ('dp', 'section')), may hold values from 0 to 191, each once within a row
- targets: bfloat16 [2, 64, 192, 256], P(None, ('dp', 'section')), may hold values from -6 to 6
Outputs:
- input_grads: bfloat16 [2, 2, 64, 48, 4096], P('grp', None, ('dp', 'section'))
- weight_grads: float32 [2, 4096, 1024], P('grp', ('dp', 'section'))
Inputs may be any that keep to these rules, and one draw needn't show every extreme that they name: Each row of order lists every one of the 192 positions once; its first 48 entries are the visible tokens, in the order of the rows of enc_input.
All inputs are finite; a program needn't handle non-finite values.
Results may differ from a plain program's by a relative error of at most 0.015.
Values may be sent and summed in bfloat16 or wider, within the bound.
A program may use at most 192 MiB of HBM per device.

v0:
```python
import math

import jax
import jax.numpy as jnp
from jax import lax
from jax.sharding import PartitionSpec as P

H = 16
HS = 64


EPS = 1e-06


def from_behind(block, axis, distance):
    devices = range(lax.axis_size(axis))
    route = [(i - distance, i) for i in devices if i - distance in devices]
    return lax.ppermute(block, axis, route)


def norm_forward(values, gain):
    rstd = lax.rsqrt(jnp.mean(values * values, axis=-1, keepdims=True) + EPS)
    return (values * rstd * gain, rstd)


def norm_backward(values, rstd, gain, upstream):
    scaled = upstream * gain
    inner = jnp.mean(scaled * values, axis=-1, keepdims=True)
    return rstd * scaled - values * (rstd * rstd * rstd) * inner


def encoder_forward(block, w_main, enc_gain, enc_bias):
    normed, rstd = norm_forward(block.astype(jnp.float32), enc_gain)
    normed_b = normed.astype(jnp.bfloat16)
    latent = (
        jnp.einsum("svc,cd->svd", normed_b, w_main, preferred_element_type=jnp.float32) + enc_bias
    )
    return (latent.astype(jnp.bfloat16), normed_b, rstd)


def encoder_backward(block, normed_b, rstd, w_main, enc_gain, d_latent, total):
    term = jnp.einsum("svc,svd->cd", normed_b, d_latent, preferred_element_type=jnp.float32)
    d_normed = jnp.einsum("svd,cd->svc", d_latent, w_main, preferred_element_type=jnp.float32)
    d_block = norm_backward(block.astype(jnp.float32), rstd, enc_gain, d_normed)
    return (d_block.astype(jnp.bfloat16), total + term)


def decoder_sample(latent, positions, target_rows, w_main, extras):
    mask_token, pos_embed, dec_gains, head_weight, head_bias = extras
    visible, width = latent.shape
    length = positions.shape[0]
    fill = jnp.broadcast_to(mask_token, (length - visible, width))
    stream = jnp.concatenate([latent.astype(jnp.float32), fill], 0) + jnp.take(
        pos_embed, positions, axis=0
    )
    normed, rstd_in = norm_forward(stream, dec_gains[0])
    act = normed.astype(jnp.bfloat16)
    stacked = w_main[: 3 * width].reshape(3, width, width)
    w_out = w_main[3 * width :]
    qkv = jnp.einsum("ti,gio->gto", act, stacked, preferred_element_type=jnp.float32).astype(
        jnp.bfloat16
    )
    heads_qkv = qkv.reshape(3, length, H, HS)
    query, keys, values = (heads_qkv[0], heads_qkv[1], heads_qkv[2])
    scale = 1.0 / math.sqrt(HS)
    scores = jnp.einsum("qhd,khd->hqk", query, keys, preferred_element_type=jnp.float32) * scale
    peak = jnp.max(scores, axis=-1, keepdims=True)
    expo = jnp.exp(scores - peak)
    probs = expo / jnp.sum(expo, axis=-1, keepdims=True)
    probs_b = probs.astype(jnp.bfloat16)
    attended = jnp.einsum("hqk,khd->qhd", probs_b, values, preferred_element_type=jnp.float32)
    attended = attended.reshape(length, width).astype(jnp.bfloat16)
    hidden = stream + jnp.dot(attended, w_out, preferred_element_type=jnp.float32)
    out_normed, rstd_out = norm_forward(hidden, dec_gains[1])
    out_b = out_normed.astype(jnp.bfloat16)
    pred = jnp.dot(out_b, head_weight, preferred_element_type=jnp.float32) + head_bias
    wanted = jnp.take(target_rows, positions, axis=0).astype(jnp.float32)
    error = (pred - wanted).astype(jnp.bfloat16)
    d_out = jnp.einsum("tp,cp->tc", error, head_weight, preferred_element_type=jnp.float32)
    d_hidden = norm_backward(hidden, rstd_out, dec_gains[1], d_out)
    d_hidden_b = d_hidden.astype(jnp.bfloat16)
    d_att = jnp.einsum("tc,ic->ti", d_hidden_b, w_out, preferred_element_type=jnp.float32).astype(
        jnp.bfloat16
    )
    d_att_h = d_att.reshape(length, H, HS)
    d_probs = jnp.einsum("qhd,khd->hqk", d_att_h, values, preferred_element_type=jnp.float32)
    d_values = jnp.einsum(
        "hqk,qhd->khd", probs_b, d_att_h, preferred_element_type=jnp.float32
    ).astype(jnp.bfloat16)
    d_scores = (
        probs * (d_probs - jnp.sum(d_probs * probs, axis=-1, keepdims=True)) * scale
    ).astype(jnp.bfloat16)
    d_query = jnp.einsum("hqk,khd->qhd", d_scores, keys, preferred_element_type=jnp.float32).astype(
        jnp.bfloat16
    )
    d_keys = jnp.einsum("hqk,qhd->khd", d_scores, query, preferred_element_type=jnp.float32).astype(
        jnp.bfloat16
    )
    d_qkv = jnp.stack([d_query, d_keys, d_values]).reshape(3, length, width)
    d_act = jnp.einsum("gto,gio->ti", d_qkv, stacked, preferred_element_type=jnp.float32)
    d_stream = d_hidden + norm_backward(stream, rstd_in, dec_gains[0], d_act)
    term_qkv = jnp.einsum("ti,gto->gio", act, d_qkv, preferred_element_type=jnp.float32).reshape(
        3 * width, width
    )
    term_out = jnp.einsum("ti,to->io", attended, d_hidden_b, preferred_element_type=jnp.float32)
    return (d_stream.astype(jnp.bfloat16), jnp.concatenate([term_qkv, term_out], 0))


def decoder_block(arrived, positions, target_rows, w_main, extras, total):
    samples, visible, width = arrived.shape

    def per_sample(carry, items):
        d_stream_b, term = decoder_sample(items[0], items[1], items[2], w_main, extras)
        return (carry + term, d_stream_b)

    total, d_streams = lax.scan(per_sample, total, (arrived, positions, target_rows))
    return (d_streams[:, :visible], d_streams.reshape(samples, visible, 4 * width), total)


def on_device(
    enc_input,
    weights,
    enc_gain,
    enc_bias,
    mask_token,
    pos_embed,
    dec_gains,
    head_weight,
    head_bias,
    order,
    targets,
):
    w_main = weights[0]
    micro, local, visible, wide = enc_input.shape
    width = w_main.shape[1]
    is_encoder = lax.axis_index("grp") == 0
    extras = (mask_token, pos_embed, dec_gains, head_weight, head_bias)
    total = jnp.zeros(w_main.shape, jnp.float32)
    blank_latent = jnp.zeros((local, visible, width), jnp.bfloat16)
    blank_normed = jnp.zeros((local, visible, wide), jnp.bfloat16)
    blank_rstd = jnp.zeros((local, visible, 1), jnp.float32)
    blanks = (blank_latent, blank_normed, blank_rstd)
    collected = []
    for step in range(micro):
        block = enc_input[step]
        latent, normed_b, rstd = lax.cond(
            is_encoder, lambda: encoder_forward(block, w_main, enc_gain, enc_bias), lambda: blanks
        )
        arrived = from_behind(latent, "grp", 1)
        d_latent, grads_dec, total = lax.cond(
            is_encoder,
            lambda: (blank_latent, blank_normed, total),
            lambda: decoder_block(arrived, order[step], targets[step], w_main, extras, total),
        )
        returned = from_behind(d_latent, "grp", -1)
        finished, total = lax.cond(
            is_encoder,
            lambda: encoder_backward(block, normed_b, rstd, w_main, enc_gain, returned, total),
            lambda: (grads_dec, total),
        )
        collected.append(finished)
    input_out = jnp.stack(collected)[None]
    dp_count = lax.axis_size("dp")
    section_count = lax.axis_size("section")
    count = micro * local * dp_count * section_count
    summed = lax.psum_scatter(total, ("dp", "section"), scatter_dimension=0, tiled=True)
    weight_out = (summed / count)[None]
    return (input_out, weight_out)


def solution(mesh):
    in_specs = (
        P(None, ("dp", "section"), None, None),
        P("grp", None, None),
        P(),
        P(),
        P(),
        P(),
        P(),
        P(),
        P(),
        P(None, ("dp", "section"), None),
        P(None, ("dp", "section"), None, None),
    )
    out_specs = (P("grp", None, ("dp", "section"), None, None), P("grp", ("dp", "section"), None))
    return jax.shard_map(
        on_device, mesh=mesh, in_specs=in_specs, out_specs=out_specs, check_vma=False
    )
```

profile of v0, /device:TPU:64, one launch (start us, length us, event | category | flops | bytes accessed | tf_op | source)
XLA Modules:
  0.0 559.9 jit_solution(6190693635490273703)
XLA Ops:
  10.6 8.3 %collective-permute-done = bf16[1,48,1024]{2,1,0:T(8,128)(2,1)S(1)} collective-permute-done((bf16[1,48,1024]{2,1,0:T(8,128)(2,1)S(1)}, bf16[1,48,1024]{2,1,0:T(8,128)(2,1)S(1)}, u32[]{:S(2)}, u32[]{:S(2)}) %collective-permute-start) | collective-permute-done | bytes 98336 | tf_op jit(solution)/shard_map/ppermute | solution.py:18
  19.0 91.3 %conditional.7 = (bf16[1,48,1024]{2,1,0:T(8,128)(2,1)}, bf16[1,48,4096]{2,1,0:T(8,128)(2,1)}, f32[4096,1024]{1,0:T(8,128)S(1)}) conditional(s32[]{:T(128)} %convert_element_type.206, (bf16[1,48,1024]{2,1,0:T(8,128)(2,1)S(1)}, f32[1024]{0:T(1024)S(1)}, s32[2,1,192]{2,1,0:T(1,128)S(1)}, f32[192,1024]{1,0:T(8,128)S(1)}, f32[2,1024]{1,0:T(2,128)S(1)}, ...), branch_computations={%region_3.13_spmd, %region_11.14_spmd} | conditional | flops 5516798464 | bytes 181401728 | solution.py:150
  23.6 3.5 slice.70
  38.4 4.8 fusion.164
  45.6 3.3 multiply_reduce_fusion.4
  59.6 3.4 convolution_convert_fusion.1
  65.0 3.5 fusion.168
  68.4 6.8 %fusion.54 = bf16[16,64,192]{2,1,0:T(8,128)(2,1)} fusion(bf16[192,16,64]{0,2,1:T(8,128)(2,1)} %bitcast.210, f32[16,192,192]{1,2,0:T(8,128)} %fusion.168, f32[16,192,192]{1,2,0:T(8,128)} %get-tuple-element.275, f32[16,192]{1,0:T(8,128)} %get-tuple-element.274), kind=kOutput, calls=%fused_computation.77 | convolution fusion | flops 79826112 | bytes 5517312 | tf_op jit(solution)/shard_map/cond/branch_0_fun/while/body/eval_jaxpr/hqk,khd->qhd/dot_general | solution.py:93
  75.2 6.9 %fusion.57 = bf16[16,64,192]{2,1,0:T(8,128)(2,1)} fusion(bf16[192,16,64]{0,2,1:T(8,128)(2,1)} %bitcast.212, f32[16,192,192]{1,2,0:T(8,128)} %fusion.168, f32[16,192,192]{1,2,0:T(8,128)} %get-tuple-element.275, f32[16,192]{1,0:T(8,128)} %get-tuple-element.274), kind=kOutput, calls=%fused_computation.78 | convolution fusion | flops 79826112 | bytes 5517312 | tf_op jit(solution)/shard_map/cond/branch_0_fun/while/body/eval_jaxpr/hqk,qhd->khd/dot_general | solution.py:96
  86.1 5.6 %multiply_reduce_fusion.2 = (f32[192]{0:T(256)S(1)}, f32[192,1024]{1,0:T(8,128)S(1)}) fusion(f32[192,1024]{1,0:T(8,128)S(1)} %gather_fusion, pred[192]{0:T(512)(128)(4,1)S(1)} %compare_and_fusion, f32[144,1024]{1,0:T(8,128)S(1)} %broadcast_in_dim.103, f32[48,1024]{1,0:T(8,128)} %bitcast_convert_fusion, f32[1024]{0:T(1024)S(1)} %bitcast.228, ...), kind=kOutput, calls=%fused_computation.92 | convolution fusion | flops 1210318592 | bytes 9835456 | tf_op jit(solution)/shard_map/cond/branch_0_fun/while/body/eval_jaxpr/gto,gio->ti/dot_general | solution.py:100
  97.6 6.5 %fusion.71 = f32[3,1024,1024]{1,2,0:T(8,128)} fusion(bf16[1,192,1024]{2,1,0:T(8,128)(2,1)S(1)} %copy-done.19, bf16[1,192,1024]{2,1,0:T(8,128)(2,1)S(1)} %copy-done.22, bf16[1,192,1024]{2,1,0:T(8,128)(2,1)S(1)} %copy-done.24, f32[1024]{0:T(1024)S(1)} %bitcast.229, f32[192]{0:T(256)S(1)} %get-tuple-element.271, f32[144,1024]{1,0:T(8,128)S(1)} %broadcast_in_dim.103, ...), kind=kOutput, calls=%fused_computation.101 | convolution fusion | flops 1210318848 | bytes 15340480 | tf_op jit(solution)/shard_map/cond/branch_0_fun/while/body/eval_jaxpr/ti,gto->gio/dot_general | solution.py:102
  104.1 6.0 %pad_maximum_fusion = f32[4096,1024]{1,0:T(8,128)S(1)} fusion(f32[1024,1024]{1,0:T(8,128)S(1)} %fusion.79, f32[3072,1024]{1,0:T(8,128)} %bitcast.190), kind=kLoop, calls=%fused_computation.58 | loop fusion | flops 4194304 | bytes 33554432 | tf_op jit(solution)/shard_map/cond/branch_0_fun/while/body/eval_jaxpr/concatenate | solution.py:106
  111.7 4.4 copy-done
  118.2 6.7 %collective-permute-done.2 = bf16[1,48,1024]{2,1,0:T(8,128)(2,1)S(1)} collective-permute-done((bf16[1,48,1024]{2,1,0:T(8,128)(2,1)S(1)}, bf16[1,48,1024]{2,1,0:T(8,128)(2,1)S(1)}, u32[]{:S(2)}, u32[]{:S(2)}) %collective-permute-start.2) | collective-permute-done | bytes 98336 | tf_op jit(solution)/shard_map/ppermute | solution.py:18
  124.9 79.3 %conditional.10 = (bf16[1,48,1024]{2,1,0:T(8,128)(2,1)S(1)}, bf16[1,48,4096]{2,1,0:T(8,128)(2,1)}, f32[4096,1024]{1,0:T(8,128)}) conditional(s32[]{:T(128)} %convert_element_type.206, (bf16[1,48,1024]{2,1,0:T(8,128)(2,1)S(1)}, f32[1024]{0:T(1024)S(1)}, s32[2,1,192]{2,1,0:T(1,128)S(1)}, f32[192,1024]{1,0:T(8,128)S(1)}, f32[2,1024]{1,0:T(2,128)S(1)}, ...), branch_computations={%region_18.28_spmd, %region_26.29_spmd} | conditional | flops 5520992768 | bytes 195033152 | solution.py:150
  127.5 3.5 slice.80
  137.7 4.3 fusion.167
  154.1 3.5 convolution_convert_fusion.4
  159.6 3.3 fusion.169
  162.9 6.8 %fusion.119 = bf16[16,64,192]{2,1,0:T(8,128)(2,1)} fusion(bf16[192,16,64]{0,2,1:T(8,128)(2,1)} %bitcast.214, f32[16,192,192]{1,2,0:T(8,128)} %fusion.169, f32[16,192,192]{1,2,0:T(8,128)} %get-tuple-element.292, f32[16,192]{1,0:T(8,128)S(1)} %get-tuple-element.291), kind=kOutput, calls=%fused_computation.154 | convolution fusion | flops 79826112 | bytes 5517312 | tf_op jit(solution)/shard_map/cond/branch_0_fun/while/body/eval_jaxpr/hqk,khd->qhd/dot_general | solution.py:93
  169.7 6.8 %fusion.122 = bf16[16,64,192]{2,1,0:T(8,128)(2,1)} fusion(bf16[192,16,64]{0,2,1:T(8,128)(2,1)} %bitcast.216, f32[16,192,192]{1,2,0:T(8,128)} %fusion.169, f32[16,192,192]{1,2,0:T(8,128)} %get-tuple-element.292, f32[16,192]{1,0:T(8,128)S(1)} %get-tuple-element.291), kind=kOutput, calls=%fused_computation.155 | convolution fusion | flops 79826112 | bytes 5517312 | tf_op jit(solution)/shard_map/cond/branch_0_fun/while/body/eval_jaxpr/hqk,qhd->khd/dot_general | solution.py:96
  180.5 5.7 %multiply_reduce_fusion.8 = (f32[192]{0:T(256)S(1)}, f32[192,1024]{1,0:T(8,128)S(1)}) fusion(f32[192,1024]{1,0:T(8,128)S(1)} %gather_fusion.2, pred[192]{0:T(512)(128)(4,1)S(1)} %compare_and_fusion.1, f32[144,1024]{1,0:T(8,128)S(1)} %broadcast_in_dim.111, f32[48,1024]{1,0:T(8,128)S(1)} %bitcast_convert_fusion.1, f32[1024]{0:T(1024)S(1)} %bitcast.231, ...), kind=kOutput, calls=%fused_computation.169 | convolution fusion | flops 1210318592 | bytes 9835456 | tf_op jit(solution)/shard_map/cond/branch_0_fun/while/body/eval_jaxpr/gto,gio->ti/dot_general | solution.py:100
  191.4 12.4 %maximum_add_fusion.3 = f32[4096,1024]{1,0:T(8,128)} fusion(f32[4096,1024]{1,0:T(8,128)} %get-tuple-element.209, f32[1024,1024]{1,0:T(8,128)S(1)} %fusion.144, f32[3072,1024]{1,0:T(8,128)S(1)} %bitcast.189), kind=kLoop, calls=%fused_computation.135 | loop fusion | flops 8388608 | bytes 50331648 | tf_op jit(solution)/shard_map/cond/branch_0_fun/while/body/eval_jaxpr/add | solution.py:114
  209.7 341.1 %reduce-scatter.2.cloned.1.call-done = f32[64,1024]{1,0:T(8,128)} async-done(((f32[4096,1024]{1,0:T(8,128)}), f32[64,1024]{1,0:T(8,128)}) %reduce-scatter.2.cloned.1.call-update) | async-done | bytes 262160 | tf_op jit(solution)/shard_map/reduce_scatter | solution.py:166
  (154 shorter events, 88.2 us)
Async XLA Ops:
  7.2 543.7 %reduce-scatter.2.cloned.1.call-start = ((), (), s32[]{:S(2)}) async-start(), calls=%async_computation.1 | async-start | bytes 17039360 | tf_op jit(solution)/shard_map/reduce_scatter | solution.py:166
  8.4 10.5 %copy-start.3 = (f32[192,1024]{1,0:T(8,128)S(1)}, f32[192,1024]{1,0:T(8,128)}, u32[]{:S(2)}) copy-start(f32[192,1024]{1,0:T(8,128)} %param.32) | copy-start | bytes 2359300
  8.4 10.5 %copy-start.6 = (bf16[1024,256]{1,0:T(8,128)(2,1)S(1)}, bf16[1024,256]{1,0:T(8,128)(2,1)}, u32[]{:S(2)}) copy-start(bf16[1024,256]{1,0:T(8,128)(2,1)} %param.34) | copy-start | bytes 1572868
  8.4 10.5 %copy-start.29 = (bf16[2,1,192,256]{3,2,1,0:T(8,128)(2,1)S(1)}, bf16[2,1,192,256]{3,2,1,0:T(8,128)(2,1)}, u32[]{:S(2)}) copy-start(bf16[2,1,192,256]{3,2,1,0:T(8,128)(2,1)} %param.37) | copy-start | bytes 589828
  8.4 10.5 %copy-start.31 = (f32[2,1024]{1,0:T(2,128)S(1)}, f32[2,1024]{1,0:T(2,128)}, u32[]{:S(2)}) copy-start(f32[2,1024]{1,0:T(2,128)} %param.33) | copy-start | bytes 24580
  8.4 10.5 %copy-start.33 = (f32[1024]{0:T(1024)S(1)}, f32[1024]{0:T(1024)}, u32[]{:S(2)}) copy-start(f32[1024]{0:T(1024)} %param.31) | copy-start | bytes 12292
  8.4 10.5 %copy-start.34 = (f32[256]{0:T(256)S(1)}, f32[256]{0:T(256)}, u32[]{:S(2)}) copy-start(f32[256]{0:T(256)} %param.35) | copy-start | bytes 3076
  8.5 10.5 %copy-start.35 = (s32[2,1,192]{2,1,0:T(1,128)S(1)}, s32[2,1,192]{2,1,0:T(1,128)}, u32[]{:S(2)}) copy-start(s32[2,1,192]{2,1,0:T(1,128)} %param.36) | copy-start | bytes 4612
  9.3 9.6 %collective-permute-start = (bf16[1,48,1024]{2,1,0:T(8,128)(2,1)S(1)}, bf16[1,48,1024]{2,1,0:T(8,128)(2,1)S(1)}, u32[]{:S(2)}, u32[]{:S(2)}) collective-permute-start(bf16[1,48,1024]{2,1,0:T(8,128)(2,1)S(1)} %get-tuple-element.235), channel_id=1, source_target_pairs={{0,1},{2,3},{4,5},{6,7},{8,9},{10,11},{12,13},{14,15},{16,17},{18,... | collective-permute-start | bytes 294920 | tf_op jit(solution)/shard_map/ppermute | solution.py:18
  19.0 92.7 %copy-start.28 = (f32[4096]{0:T(1024)S(1)}, f32[4096]{0:T(1024)}, u32[]{:S(2)}) copy-start(f32[4096]{0:T(1024)} %param.29) | copy-start | bytes 49156
  19.0 92.7 %copy-start.32 = (f32[1024]{0:T(1024)S(1)}, f32[1024]{0:T(1024)}, u32[]{:S(2)}) copy-start(f32[1024]{0:T(1024)} %param.30) | copy-start | bytes 12292
  23.6 6.2 %copy-start.9 = (f32[48,1024]{1,0:T(8,128)S(1)}, f32[48,1024]{1,0:T(8,128)}, u32[]{:S(2)}) copy-start(f32[48,1024]{1,0:T(8,128)} %bitcast_convert_fusion) | copy-start | bytes 589828 | tf_op jit(solution)/shard_map/cond
  27.2 2.7 copy-start.4
  45.6 3.3 copy-start.26
  86.1 5.7 %copy-start.8 = (f32[192,1024]{1,0:T(8,128)S(1)}, f32[192,1024]{1,0:T(8,128)}, u32[]{:S(2)}) copy-start(f32[192,1024]{1,0:T(8,128)} %copy-done.7) | copy-start | bytes 2359300 | tf_op jit(solution)/shard_map/cond
  86.1 5.7 %copy-start.11 = (f32[48,1024]{1,0:T(8,128)S(1)}, f32[48,1024]{1,0:T(8,128)}, u32[]{:S(2)}) copy-start(f32[48,1024]{1,0:T(8,128)} %bitcast_convert_fusion) | copy-start | bytes 589828 | tf_op jit(solution)/shard_map/cond
  110.3 5.7 %copy-start = (f32[4096,1024]{1,0:T(8,128)}, f32[4096,1024]{1,0:T(8,128)S(1)}, u32[]{:S(2)}) copy-start(f32[4096,1024]{1,0:T(8,128)S(1)} %get-tuple-element.333) | copy-start | bytes 50331652
  110.3 7.8 %collective-permute-start.1 = (bf16[1,48,1024]{2,1,0:T(8,128)(2,1)}, bf16[1,48,1024]{2,1,0:T(8,128)(2,1)S(1)}, u32[]{:S(2)}, u32[]{:S(2)}) collective-permute-start(bf16[1,48,1024]{2,1,0:T(8,128)(2,1)} %get-tuple-element.239), channel_id=1, source_target_pairs={{1,0},{3,2},{5,4},{7,6},{9,8},{11,10},{13,12},{15,14},{17,16},{19,... | collective-permute-start | bytes 294920 | tf_op jit(solution)/shard_map/ppermute | solution.py:18
  116.9 8.0 %collective-permute-start.2 = (bf16[1,48,1024]{2,1,0:T(8,128)(2,1)S(1)}, bf16[1,48,1024]{2,1,0:T(8,128)(2,1)S(1)}, u32[]{:S(2)}, u32[]{:S(2)}) collective-permute-start(bf16[1,48,1024]{2,1,0:T(8,128)(2,1)S(1)} %get-tuple-element.242), channel_id=1, source_target_pairs={{0,1},{2,3},{4,5},{6,7},{8,9},{10,11},{12,13},{14,15},{16,17},{18,... | collective-permute-start | bytes 294920 | tf_op jit(solution)/shard_map/ppermute | solution.py:18
  118.2 6.7 %copy-start.30 = (bf16[2,1,192,256]{3,2,1,0:T(8,128)(2,1)S(1)}, bf16[2,1,192,256]{3,2,1,0:T(8,128)(2,1)}, u32[]{:S(2)}) copy-start(bf16[2,1,192,256]{3,2,1,0:T(8,128)(2,1)} %param.37) | copy-start | bytes 589828
  137.7 6.7 %copy-start.14 = (bf16[1,192,1024]{1,2,0:T(8,128)(2,1)}, bf16[1,192,1024]{1,2,0:T(8,128)(2,1)S(1)}, u32[]{:S(2)}) copy-start(bf16[1,192,1024]{1,2,0:T(8,128)(2,1)S(1)} %copy.56) | copy-start | bytes 1179652 | tf_op jit(solution)/shard_map/cond
  154.1 5.5 copy-start.15
  169.7 10.8 %copy-start.20 = (bf16[1,192,1024]{2,1,0:T(8,128)(2,1)S(1)}, bf16[1,192,1024]{2,1,0:T(8,128)(2,1)}, u32[]{:S(2)}) copy-start(bf16[1,192,1024]{2,1,0:T(8,128)(2,1)} %copy.66) | copy-start | bytes 1179652 | tf_op jit(solution)/shard_map/cond
  204.2 3.5 collective-permute-start.3
  (15 other events, 25.3 us)
Sparse Core Ops, SparseCore 0:
  207.8 343.0 reduce-scatter.1
where the time goes:
time: 571 us; the launch traced here: 560 us
  waiting for transfers between devices  358 us (63%)
  matrix products  97.4 us (17%)
  local copies, waits for them, and re-layouts  55.9 us (10%)
  other arithmetic  27 us (5%)
  between operations  14.8 us (3%)
    reduce_scatter x1, waiting for transfers between devices, on_device(): lax.psum_scatter(total, ('dp', 'section'), scatter_dimension=0, tiled=True)  341 us
    ppermute x4, waiting for transfers between devices, from_behind(): return lax.ppermute(block, axis, route)  17.2 us
    dot_general x2, matrix products, decoder_sample(): jnp.einsum('hqk,qhd->khd', d_scores, query, preferred_element_type=jnp.fl...  13.7 us
    dot_general x2, matrix products, decoder_sample(): jnp.einsum('hqk,khd->qhd', d_scores, keys, preferred_element_type=jnp.flo...  13.6 us
    add x1, other arithmetic, per_sample(): return (carry + term, d_stream_b)  12.4 us
    another operation x6, local copies, waits for them, and re-layouts, decoder_sample(): d_qkv = jnp.stack([d_query, d_keys, d_values]).reshape(3, length, width)  11.9 us
  transfers between devices with their start and end apart: 5, of which 4 were waited for; matrix products, arithmetic and copies ran while one was open for 0% of the time, Pallas kernels for 0%

commit v1 on v0

v1 whole, which is shorter than its diff:
```python
import functools
import math

import jax
import jax.numpy as jnp
from jax import lax
from jax.experimental import pallas as pl
from jax.experimental.pallas import tpu as pltpu
from jax.sharding import PartitionSpec as P

MESH = pl.DeviceIdType.MESH
B16 = jnp.bfloat16
F32 = jnp.float32
EPS = 1e-06
D = 1024
DE = 4096
L = 192
VIS = 48
HS = 64
ROWS = 2 * L
GROUP = 256
HEADS = GROUP // HS
NT = (((1,), (1,)), ((), ()))
TN = (((0,), (0,)), ((), ()))


def nn(a, b):
    return jnp.dot(a, b, preferred_element_type=F32)


def nt(a, b):
    return lax.dot_general(a, b, NT, preferred_element_type=F32)


def tn(a, b):
    return lax.dot_general(a, b, TN, preferred_element_type=F32)


def loop(n, body, unroll=1):
    def step(i, carry):
        body(i)
        return carry

    lax.fori_loop(0, n, step, 0, unroll=unroll)


def span(i, size):
    return pl.ds(pl.multiple_of(i * size, size), size)


def head_mask(h):
    return lax.broadcasted_iota(jnp.int32, (L, GROUP), 1) // HS == h


def stack_heads(block):
    zero = jnp.zeros_like(block)
    return jnp.concatenate([jnp.where(head_mask(h), block, zero) for h in range(HEADS)], 0)


def fold_heads(block):
    out = jnp.where(head_mask(0), block[:L], 0.0)
    for h in range(1, HEADS):
        out = jnp.where(head_mask(h), block[h * L : (h + 1) * L], out)
    return out


def norm_rows(values, gain):
    rstd = lax.rsqrt(jnp.mean(values * values, axis=-1, keepdims=True) + EPS)
    return values * rstd * gain


def norm_rows_back(values, gain, upstream):
    rstd = lax.rsqrt(jnp.mean(values * values, axis=-1, keepdims=True) + EPS)
    scaled = upstream * gain
    inner = jnp.mean(scaled * values, axis=-1, keepdims=True)
    return rstd * scaled - values * (rstd * rstd * rstd) * inner


class Ax:
    def __init__(self, view, r1, r2, ss, rs, plus, minus, send):
        self.view, self.r1, self.r2 = view, r1, r2
        self.ss, self.rs, self.plus, self.minus, self.send = ss, rs, plus, minus, send

    def half(self, ref, h):
        n = ref.shape[0] // 2
        return ref.at[pl.ds(h * n, n)]

    def go(self, src, dst, k, who):
        return self.send(src, dst, self.ss.at[k], self.rs.at[k], who)

    def step1(self):
        self.c0 = self.go(self.half(self.view(0), 0), self.r1.at[0], 0, self.plus)
        self.c1 = self.go(self.half(self.view(0), 1), self.r1.at[1], 1, self.minus)

    def step2(self):
        self.c2 = self.go(self.half(self.view(1), 1), self.half(self.r2.at[0], 1), 2, self.plus)
        self.c3 = self.go(self.half(self.view(2), 0), self.half(self.r2.at[1], 0), 3, self.minus)

    def step3(self):
        self.c0.wait_recv()
        mine = self.half(self.view(1), 0)
        mine[...] = mine[...] + self.r1[0]
        self.c4 = self.go(mine, self.half(self.r2.at[0], 0), 4, self.plus)
        self.c1.wait_recv()
        mine = self.half(self.view(2), 1)
        mine[...] = mine[...] + self.r1[1]
        self.c5 = self.go(mine, self.half(self.r2.at[1], 1), 5, self.minus)

    def finish_waits(self):
        for copy in (self.c2, self.c3, self.c4, self.c5):
            copy.wait_recv()


def kernel(
    scale,
    x_hbm, w_hbm, enc_gain, enc_bias, mask_token, pos_hbm, dec_gains, head_hbm, head_bias, order, tgt_hbm,
    g_out, w_out,
    w, pos, head, tgt, lat, lat_in, dlat, dlat_in,
    xb, normed, normed_t, rstd, acc, d_norm,
    stream, hidden, d_hidden, d_stream, tall, act, q, k, v, att, out_b, d_att, back, at, probs, wanted, err, gbuf,
    term, core_x, core_y, r1_x, r1_y, r2_x, r2_y, acc2_x, acc2_y, s1_x, s1_y, s2_x, s2_y, zr,
    w_sem, in_sem, out_sem, grp_send, grp_recv,
    core_send, core_recv, ssem, rsem, ssem2, rsem2, zsend, zrecv,
):
    dp = lax.axis_index("dp")
    x = lax.axis_index("section")
    grp = lax.axis_index("grp")
    y = dp // 4
    z = (dp // 2) % 2
    c = dp % 2

    def at_y(t):
        return {"dp": t * 4 + z * 2 + c}

    def at_x(t):
        return {"section": t}

    to_core = {"dp": y * 4 + z * 2 + (1 - c)}
    to_z = {"dp": y * 4 + (1 - z) * 2 + c}
    to_grp = {"grp": 1 - grp}
    xs = [(x + 2) % 4, (x + 1) % 4, (x + 3) % 4, x]
    ys = [(y + 2) % 4, (y + 1) % 4, (y + 3) % 4, y]

    barrier = pltpu.get_barrier_semaphore()
    for who in (to_grp, to_core, to_z, at_x(xs[1]), at_x(xs[2]), at_y(ys[1]), at_y(ys[2])):
        pl.semaphore_signal(barrier, inc=1, device_id=who, device_id_type=MESH)

    def remote(src, dst, send, recv, who):
        return pltpu.make_async_remote_copy(
            src_ref=src, dst_ref=dst, send_sem=send, recv_sem=recv, device_id=who, device_id_type=MESH
        )

    def w_copy(i):
        rows = pl.ds(pl.multiple_of(i * 512, 512), 512)
        return pltpu.make_async_copy(w_hbm.at[rows], w.at[rows], w_sem.at[i])

    x_copy = pltpu.make_async_copy(x_hbm, xb, in_sem.at[0])
    pos_copy = pltpu.make_async_copy(pos_hbm, pos, in_sem.at[1])
    head_copy = pltpu.make_async_copy(head_hbm, head, in_sem.at[2])
    tgt_copy = pltpu.make_async_copy(tgt_hbm, tgt, in_sem.at[3])
    lat_copy = remote(lat, lat_in, grp_send.at[0], grp_recv.at[0], to_grp)
    dlat_copy = remote(dlat, dlat_in, grp_send.at[1], grp_recv.at[1], to_grp)
    g_copy = pltpu.make_async_copy(gbuf, g_out, out_sem.at[0])

    @pl.when(grp == 0)
    def _():
        x_copy.start()

    @pl.when(grp == 1)
    def _():
        pos_copy.start()

    for i in range(8):
        w_copy(i).start()

    @pl.when(grp == 0)
    def _():
        x_copy.wait()
        squares = jnp.zeros((2 * VIS, 128), F32)
        for j in range(DE // 128):
            part = xb[:, j * 128 : (j + 1) * 128].astype(F32)
            squares = squares + part * part
        rs = lax.rsqrt(jnp.sum(squares, axis=-1, keepdims=True) * (1.0 / DE) + EPS)
        rstd[...] = jnp.broadcast_to(rs, (2 * VIS, 128))
        acc[...] = jnp.broadcast_to(enc_bias[...], (2 * VIS, D))

        def step(i):
            cols = span(i, 512)
            block = xb[:, cols].astype(F32) * rstd[:, 0:1] * enc_gain[:, cols]
            block = block.astype(B16)
            normed[:, cols] = block
            w_copy(i).wait()
            acc[...] += nn(block, w[cols, :])

        loop(8, step)
        lat[...] = acc[...].astype(B16)

    @pl.when(grp == 1)
    def _():
        tgt_copy.start()
        head_copy.start()
        pos_copy.wait()

        def onehot(s):
            rows = lax.broadcasted_iota(jnp.int32, (L, L), 0)
            return jnp.where(rows == order[s, 0:1, :], 1.0, 0.0).astype(B16)

        for s in range(2):
            hot = onehot(s)

            def gather(i):
                cols = span(i, 256)
                table = pos[:, cols]
                hi = table.astype(B16)
                rest = table - hi.astype(F32)
                mid = rest.astype(B16)
                low = (rest - mid.astype(F32)).astype(B16)
                rows = (tn(hot, hi) + tn(hot, mid)) + tn(hot, low)
                stream[s * L : s * L + VIS, cols] = rows[:VIS]
                stream[s * L + VIS : (s + 1) * L, cols] = rows[VIS:] + mask_token[:, cols]

            loop(4, gather)
        tgt_copy.wait()
        for s in range(2):
            wanted[s * L : (s + 1) * L, :] = tn(onehot(s), tgt[s]).astype(B16)
        gain = dec_gains[0:1, :]
        for s in range(2):

            def norms(i):
                rows = pl.ds(pl.multiple_of(s * L + VIS + i * 48, 16), 48)
                act[rows, :] = norm_rows(stream[rows, :], gain).astype(B16)

            loop(3, norms)
        for i in range(6):
            w_copy(i).wait()
        for part, dst in enumerate((q, k, v)):
            for s in range(2):

                def project(i):
                    cols = span(i, 256)
                    rows = pl.ds(s * L + VIS, L - VIS)
                    dst[rows, cols] = nn(act[rows, :], w[part * D : (part + 1) * D, cols]).astype(B16)

                loop(4, project)
        for i in range(6, 8):
            w_copy(i).wait()
        head_copy.wait()

    pl.semaphore_wait(barrier, 7)

    @pl.when(grp == 0)
    def _():
        lat_copy.start()

        def flip(i):
            cols = span(i, 512)
            normed_t[cols, :] = normed[:, cols].T

        loop(8, flip)
        lat_copy.wait_send()

    @pl.when(grp == 1)
    def _():
        lat_copy.wait_recv()
        gain = dec_gains[0:1, :]
        for s in range(2):
            rows = slice(s * L, s * L + VIS)
            value = stream[rows, :] + lat_in[s * VIS : (s + 1) * VIS, :].astype(F32)
            stream[rows, :] = value
            act[rows, :] = norm_rows(value, gain).astype(B16)
        for part, dst in enumerate((q, k, v)):

            def project(i):
                cols = span(i, 256)
                both = jnp.concatenate([act[:VIS, :], act[L : L + VIS, :]], 0)
                value = nn(both, w[part * D : (part + 1) * D, cols]).astype(B16)
                dst[:VIS, cols] = value[:VIS]
                dst[L : L + VIS, cols] = value[VIS:]

            loop(4, project)

        shrink = 1.0 / math.sqrt(HS)

        def attend(i):
            rows = span(i // 4, L)
            cols = span(i % 4, GROUP)
            scores = nt(stack_heads(q[rows, cols]), k[rows, cols]) * shrink
            expo = jnp.exp(scores - jnp.max(scores, axis=-1, keepdims=True))
            p = expo / jnp.sum(expo, axis=-1, keepdims=True)
            probs[i] = p
            att[rows, cols] = fold_heads(nn(p.astype(B16), v[rows, cols])).astype(B16)

        loop(8, attend)

        def out_proj(i):
            cols = span(i, 256)
            hidden[:, cols] = stream[:, cols] + nn(att[...], w[3 * D :, cols])

        loop(4, out_proj)
        gain_out = dec_gains[1:2, :]

        def out_norm(i):
            rows = span(i, 48)
            out_b[rows, :] = norm_rows(hidden[rows, :], gain_out).astype(B16)

        loop(8, out_norm)

        def pixel_head(i):
            rows = span(i, L)
            pred = nn(out_b[rows, :], head[...]) + head_bias[...]
            err[rows, :] = (pred - wanted[rows, :].astype(F32)).astype(B16)

        loop(2, pixel_head)

        def head_back(i):
            rows = span(i, 96)
            d_out = nt(err[rows, :], head[...])
            value = norm_rows_back(hidden[rows, :], gain_out, d_out)
            d_hidden[rows, :] = value
            back[3, rows, :] = value.astype(B16)

        loop(4, head_back)

        def att_back(i):
            cols = span(i, 256)
            d_att[:, cols] = nt(back[3], w[pl.ds(pl.multiple_of(3 * D + i * 256, 256), 256), :]).astype(B16)

        loop(4, att_back)

        def attend_back(i):
            rows = span(i // 4, L)
            cols = span(i % 4, GROUP)
            p = probs[i]
            up = stack_heads(d_att[rows, cols])
            d_p = nt(up, v[rows, cols])
            d_s = p * (d_p - jnp.sum(d_p * p, axis=-1, keepdims=True)) * shrink
            d_s = d_s.astype(B16)
            back[2, rows, cols] = tn(p.astype(B16), up).astype(B16)
            back[0, rows, cols] = fold_heads(nn(d_s, k[rows, cols])).astype(B16)
            back[1, rows, cols] = tn(d_s, stack_heads(q[rows, cols])).astype(B16)

        loop(8, attend_back)

        def act_back(i):
            cols = span(i, 256)
            total = nt(back[0], w[pl.ds(pl.multiple_of(i * 256, 256), 256), :])
            total = total + nt(back[1], w[pl.ds(pl.multiple_of(D + i * 256, 256), 256), :])
            total = total + nt(back[2], w[pl.ds(pl.multiple_of(2 * D + i * 256, 256), 256), :])
            d_stream[:, cols] = total

        loop(4, act_back)

        def stream_back(i):
            rows = span(i, 48)
            value = d_hidden[rows, :] + norm_rows_back(stream[rows, :], gain, d_stream[rows, :])
            for t in range(8):
                tall[t, rows, :] = value[:, t * 128 : (t + 1) * 128]

            @pl.when(i % 4 == 0)
            def _():
                dlat[span(i // 4, VIS), :] = value.astype(B16)

        loop(8, stream_back)
        dlat_copy.start()
        at[0] = act[...].T
        at[1] = att[...].T

        def terms(i):
            blk = i // 4
            value = nn(at[blk // 3, span(i % 4, 256), :], back[blk])
            term[i // 4, (i // 2) % 2, i % 2] = value.astype(B16).reshape(4, 64, D)

        loop(16, terms)
        for s in range(2):
            for j in range(4):
                for t in range(8):
                    start = j * D + t * 128
                    gbuf[s, :, start : start + 128] = tall[t, pl.ds(s * L + j, VIS, stride=4), :].astype(B16)
        g_copy.start()
        dlat_copy.wait_send()

    @pl.when(grp == 0)
    def _():
        dlat_copy.wait_recv()

        def terms(i):
            value = nn(normed_t[span(i, 256), :], dlat_in[...])
            term[i // 4, (i // 2) % 2, i % 2] = value.astype(B16).reshape(4, 64, D)

        loop(16, terms)

    def send(src, dst, send_s, recv_s, who):
        copy = remote(src, dst, send_s, recv_s, who)
        copy.start()
        started.append(copy)
        return copy

    started = []

    def px(j, core):
        return term.at[:, :, core, xs[j], pl.ds(0, 32)]

    def py(j, core):
        return term.at[ys[j], :, core, :, pl.ds(32, 32)]

    parts = (px, py)
    corebufs = (core_x, core_y)
    cores = {}
    for a, j in ((0, 0), (1, 0), (0, 1), (0, 2), (1, 1), (1, 2), (0, 3), (1, 3)):
        cores[a, j] = send(
            parts[a](j, 1 - c), corebufs[a].at[j], core_send.at[a, j], core_recv.at[a, j], to_core
        )

    def merge(a, j):
        cores[a, j].wait_recv()
        mine = parts[a](j, c)
        mine[...] = mine[...] + corebufs[a][j]

    first = (
        Ax(lambda j: px(j, c), r1_x, r2_x, ssem.at[0], rsem.at[0], at_x(xs[1]), at_x(xs[2]), send),
        Ax(lambda j: py(j, c), r1_y, r2_y, ssem.at[1], rsem.at[1], at_y(ys[1]), at_y(ys[2]), send),
    )
    second = (
        Ax(lambda j: acc2_x.at[j], s1_x, s2_x, ssem2.at[0], rsem2.at[0], at_y(ys[1]), at_y(ys[2]), send),
        Ax(lambda j: acc2_y.at[j], s1_y, s2_y, ssem2.at[1], rsem2.at[1], at_x(xs[1]), at_x(xs[2]), send),
    )
    for a in (0, 1):
        merge(a, 0)
        first[a].step1()
    for a in (0, 1):
        merge(a, 1)
        merge(a, 2)
        first[a].step2()
    @pl.when(grp == 0)
    def _():
        acc2 = jnp.zeros((2 * VIS, 1), F32)

        def step(i, inner):
            cols = span(i, 256)
            d_n = nt(dlat_in[...], w[cols, :])
            scaled = d_n * enc_gain[:, cols]
            d_norm[:, cols] = scaled
            return inner + jnp.sum(scaled * xb[:, cols].astype(F32), axis=-1, keepdims=True)

        inner = lax.fori_loop(0, 16, step, acc2) * (1.0 / DE)
        rs = rstd[:, 0:1]
        factor = rs * rs * rs * inner
        for i in range(8):
            cols = slice(i * 512, (i + 1) * 512)
            value = (rs * d_norm[:, cols] - xb[:, cols].astype(F32) * factor).astype(B16)
            gbuf[0, :, cols] = value[:VIS]
            gbuf[1, :, cols] = value[VIS:]
        g_copy.start()

    for a in (0, 1):
        first[a].step3()
    for a in (0, 1):
        merge(a, 3)

    def total(a, j):
        ax = first[a]
        if a == 0:
            rows = lambda ref: ref[ys[j]]
        else:
            rows = lambda ref: ref[:, xs[j]]
        value = rows(ax.view(3)).astype(F32) + rows(ax.r2.at[0]).astype(F32) + rows(ax.r2.at[1]).astype(F32)
        second[a].view(j)[...] = value.astype(B16)

    for a in (0, 1):
        first[a].finish_waits()
        total(a, 0)
        second[a].step1()
        total(a, 1)
        total(a, 2)
        second[a].step2()
        total(a, 3)
    for a in (0, 1):
        second[a].step3()
    zcopies = []
    for a in (0, 1):
        ax = second[a]
        ax.finish_waits()
        mine = ax.view(3)
        value = mine[...].astype(F32) + ax.r2[0].astype(F32) + ax.r2[1].astype(F32)
        mine[...] = value.astype(B16)
        zcopies.append(send(mine.at[1 - z], zr.at[a], zsend.at[a], zrecv.at[a], to_z))
    for a in (0, 1):
        zcopies[a].wait_recv()
        w_out[a * 32 : (a + 1) * 32, :] = (second[a].view(3)[z].astype(F32) + zr[a].astype(F32)) * scale
    g_copy.wait()
    for copy in started:
        copy.wait_send()


def on_device(
    enc_input, weights, enc_gain, enc_bias, mask_token, pos_embed, dec_gains, head_weight, head_bias, order, targets
):
    V = pltpu.VMEM
    S = pltpu.SemaphoreType.DMA
    full = pl.BlockSpec(memory_space=pltpu.VMEM)
    hbm = pl.BlockSpec(memory_space=pl.ANY)
    count = 2 * lax.axis_size("dp") * lax.axis_size("section")
    grads, w_grad = pl.pallas_call(
        functools.partial(kernel, 1.0 / count),
        out_shape=(jax.ShapeDtypeStruct((2, VIS, DE), B16), jax.ShapeDtypeStruct((64, D), F32)),
        in_specs=[hbm, hbm, full, full, full, hbm, full, hbm, full, full, hbm],
        out_specs=(hbm, full),
        scratch_shapes=[
            V((DE, D), B16), V((L, D), F32), V((D, 256), B16), V((2, L, 256), B16),
            V((2 * VIS, D), B16), V((2 * VIS, D), B16), V((2 * VIS, D), B16), V((2 * VIS, D), B16),
            V((2 * VIS, DE), B16), V((2 * VIS, DE), B16), V((DE, 2 * VIS), B16), V((2 * VIS, 128), F32),
            V((2 * VIS, D), F32), V((2 * VIS, DE), F32),
            V((ROWS, D), F32), V((ROWS, D), F32), V((ROWS, D), F32), V((ROWS, D), F32), V((8, ROWS, 128), F32),
            V((ROWS, D), B16), V((ROWS, D), B16), V((ROWS, D), B16), V((ROWS, D), B16), V((ROWS, D), B16),
            V((ROWS, D), B16), V((ROWS, D), B16), V((4, ROWS, D), B16), V((2, D, ROWS), B16),
            V((8, HEADS * L, L), F32), V((ROWS, 256), B16), V((ROWS, 256), B16), V((2, VIS, DE), B16),
            V((4, 2, 2, 4, 64, D), B16),
            V((4, 4, 2, 32, D), B16), V((4, 2, 4, 32, D), B16),
            V((2, 2, 2, 32, D), B16), V((2, 1, 4, 32, D), B16),
            V((2, 4, 2, 32, D), B16), V((2, 2, 4, 32, D), B16),
            V((4, 2, 32, D), B16), V((4, 2, 32, D), B16),
            V((2, 1, 32, D), B16), V((2, 1, 32, D), B16),
            V((2, 2, 32, D), B16), V((2, 2, 32, D), B16),
            V((2, 32, D), B16),
            S((8,)), S((4,)), S((1,)), S((2,)), S((2,)),
            S((2, 4)), S((2, 4)), S((2, 6)), S((2, 6)), S((2, 6)), S((2, 6)), S((2,)), S((2,)),
        ],
        compiler_params=pltpu.CompilerParams(
            collective_id=0, has_side_effects=True, vmem_limit_bytes=60 * 2**20
        ),
        name="window",
    )(
        enc_input.reshape(2 * VIS, DE), weights[0], enc_gain[None], enc_bias[None], mask_token[None], pos_embed,
        dec_gains, head_weight, head_bias[None], order, targets.reshape(2, L, 256),
    )
    return grads[None, :, None], w_grad[None]


def solution(mesh):
    many = ("dp", "section")
    in_specs = (
        P(None, many, None, None), P("grp", None, None), P(), P(), P(), P(), P(), P(), P(),
        P(None, many, None), P(None, many, None, None),
    )
    out_specs = (P("grp", None, many, None, None), P("grp", many, None))
    return jax.shard_map(on_device, mesh=mesh, in_specs=in_specs, out_specs=out_specs, check_vma=False)
```

time: 571 us -> 93.8 us (0.16)
  the two profiles are of different devices: /device:TPU:64 before, /device:TPU:0 now
where the time goes in v1:
time: 93.8 us; the launch traced here: 93.5 us
  Pallas kernels  89.2 us (95%)
  local copies, waits for them, and re-layouts  3.73 us (4%)
    pallas_call x1, Pallas kernels, on_device(): pl.pallas_call(functools.partial(kernel, 1.0 / count), out_shape=(jax.Sha...  89.2 us
    unnamed x2, local copies, waits for them, and re-layouts  3.73 us

profile of v1, /device:TPU:0, one launch (start us, length us, event | category | flops | bytes accessed | tf_op | source)
XLA Modules:
  0.0 93.5 jit_solution(6813040206328557989)
XLA Ops:
  0.6 89.2 %window.1 = (bf16[2,48,4096]{2,1,0:T(8,128)(2,1)}, f32[64,1024]{1,0:T(8,128)}) custom-call(bf16[96,4096]{1,0:T(8,128)(2,1)} %bitcast.12, bf16[4096,1024]{1,0:T(8,128)(2,1)} %bitcast.11, f32[1,4096]{1,0:T(1,128)} %bitcast.16, f32[1,1024]{1,0:T(1,128)} %bitcast.17, f32[1,1024]{1,0:T(1,128)} %bitcast.18, f32[192,1024]{1,0:T(8,128)} %pos_hbm.1, ...), custom_call_target="tpu_custom_call" | custom-call | tf_op jit(solution)/shard_map/window/pallas_call | solution.py:503
  89.8 2.1 %copy.16 = bf16[1,2,1,48,4096]{4,3,2,1,0:T(8,128)(2,1)} copy(bf16[1,2,1,48,4096]{4,3,2,1,0:T(8,128)(2,1)} %bitcast.13) | data formatting | bytes 1572864
  91.9 1.7 %copy.17 = f32[1,64,1024]{2,1,0:T(8,128)} copy(f32[1,64,1024]{2,1,0:T(8,128)} %bitcast.14) | data formatting | bytes 524288

commit v2 on v1

--- a/solution.py
+++ b/solution.py
@@ -117,7 +117,7 @@
     g_out, w_out,
     w, pos, head, tgt, lat, lat_in, dlat, dlat_in,
     xb, normed, normed_t, rstd, acc, d_norm,
-    stream, hidden, d_hidden, d_stream, tall, act, q, k, v, att, out_b, d_att, back, at, probs, wanted, err, gbuf,
+    stream, hidden, d_hidden, d_stream, tall, act, act_m, act_v, q, k, v, att, out_b, d_att, back, at, probs, wanted, err, gbuf,
     term, core_x, core_y, r1_x, r1_y, r2_x, r2_y, acc2_x, acc2_y, s1_x, s1_y, s2_x, s2_y, zr,
     w_sem, in_sem, out_sem, grp_send, grp_recv,
     core_send, core_recv, ssem, rsem, ssem2, rsem2, zsend, zrecv,
@@ -192,7 +192,7 @@
             w_copy(i).wait()
             acc[...] += nn(block, w[cols, :])
 
-        loop(8, step)
+        loop(8, step, 8)
         lat[...] = acc[...].astype(B16)
 
     @pl.when(grp == 1)
@@ -201,47 +201,32 @@
         head_copy.start()
         pos_copy.wait()
 
-        def onehot(s):
+        hi = pos[...].astype(B16)
+        rest = pos[...] - hi.astype(F32)
+        mid = rest.astype(B16)
+        low = (rest - mid.astype(F32)).astype(B16)
+        gain = dec_gains[0:1, :]
+        hots = []
+        for s in range(2):
             rows = lax.broadcasted_iota(jnp.int32, (L, L), 0)
-            return jnp.where(rows == order[s, 0:1, :], 1.0, 0.0).astype(B16)
-
-        for s in range(2):
-            hot = onehot(s)
-
-            def gather(i):
-                cols = span(i, 256)
-                table = pos[:, cols]
-                hi = table.astype(B16)
-                rest = table - hi.astype(F32)
-                mid = rest.astype(B16)
-                low = (rest - mid.astype(F32)).astype(B16)
-                rows = (tn(hot, hi) + tn(hot, mid)) + tn(hot, low)
-                stream[s * L : s * L + VIS, cols] = rows[:VIS]
-                stream[s * L + VIS : (s + 1) * L, cols] = rows[VIS:] + mask_token[:, cols]
-
-            loop(4, gather)
+            hot = jnp.where(rows == order[s, 0:1, :], 1.0, 0.0).T.astype(B16)
+            hots.append(hot)
+            found = (nn(hot, hi) + nn(hot, mid)) + nn(hot, low)
+            stream[s * L : s * L + VIS, :] = found[:VIS]
+            value = found[VIS:] + mask_token[...]
+            stream[s * L + VIS : (s + 1) * L, :] = value
+            normal = norm_rows(value, gain).astype(B16)
+            act[s * L + VIS : (s + 1) * L, :] = normal
+            act_m[s * (L - VIS) : (s + 1) * (L - VIS), :] = normal
+        for part, dst in enumerate((q, k, v)):
+            w_copy(2 * part).wait()
+            w_copy(2 * part + 1).wait()
+            value = nn(act_m[...], w[part * D : (part + 1) * D, :]).astype(B16)
+            dst[VIS:L, :] = value[: L - VIS]
+            dst[L + VIS :, :] = value[L - VIS :]
         tgt_copy.wait()
         for s in range(2):
-            wanted[s * L : (s + 1) * L, :] = tn(onehot(s), tgt[s]).astype(B16)
-        gain = dec_gains[0:1, :]
-        for s in range(2):
-
-            def norms(i):
-                rows = pl.ds(pl.multiple_of(s * L + VIS + i * 48, 16), 48)
-                act[rows, :] = norm_rows(stream[rows, :], gain).astype(B16)
-
-            loop(3, norms)
-        for i in range(6):
-            w_copy(i).wait()
-        for part, dst in enumerate((q, k, v)):
-            for s in range(2):
-
-                def project(i):
-                    cols = span(i, 256)
-                    rows = pl.ds(s * L + VIS, L - VIS)
-                    dst[rows, cols] = nn(act[rows, :], w[part * D : (part + 1) * D, cols]).astype(B16)
-
-                loop(4, project)
+            wanted[s * L : (s + 1) * L, :] = nn(hots[s], tgt[s]).astype(B16)
         for i in range(6, 8):
             w_copy(i).wait()
         head_copy.wait()
@@ -256,7 +241,7 @@
             cols = span(i, 512)
             normed_t[cols, :] = normed[:, cols].T
 
-        loop(8, flip)
+        loop(8, flip, 4)
         lat_copy.wait_send()
 
     @pl.when(grp == 1)
@@ -267,17 +252,13 @@
             rows = slice(s * L, s * L + VIS)
             value = stream[rows, :] + lat_in[s * VIS : (s + 1) * VIS, :].astype(F32)
             stream[rows, :] = value
-            act[rows, :] = norm_rows(value, gain).astype(B16)
+            normal = norm_rows(value, gain).astype(B16)
+            act[rows, :] = normal
+            act_v[s * VIS : (s + 1) * VIS, :] = normal
         for part, dst in enumerate((q, k, v)):
-
-            def project(i):
-                cols = span(i, 256)
-                both = jnp.concatenate([act[:VIS, :], act[L : L + VIS, :]], 0)
-                value = nn(both, w[part * D : (part + 1) * D, cols]).astype(B16)
-                dst[:VIS, cols] = value[:VIS]
-                dst[L : L + VIS, cols] = value[VIS:]
-
-            loop(4, project)
+            value = nn(act_v[...], w[part * D : (part + 1) * D, :]).astype(B16)
+            dst[:VIS, :] = value[:VIS]
+            dst[L : L + VIS, :] = value[VIS:]
 
         shrink = 1.0 / math.sqrt(HS)
 
@@ -286,46 +267,26 @@
             cols = span(i % 4, GROUP)
             scores = nt(stack_heads(q[rows, cols]), k[rows, cols]) * shrink
             expo = jnp.exp(scores - jnp.max(scores, axis=-1, keepdims=True))
-            p = expo / jnp.sum(expo, axis=-1, keepdims=True)
+            p = expo * (1.0 / jnp.sum(expo, axis=-1, keepdims=True))
             probs[i] = p
             att[rows, cols] = fold_heads(nn(p.astype(B16), v[rows, cols])).astype(B16)
 
-        loop(8, attend)
-
-        def out_proj(i):
-            cols = span(i, 256)
-            hidden[:, cols] = stream[:, cols] + nn(att[...], w[3 * D :, cols])
-
-        loop(4, out_proj)
+        loop(8, attend, 8)
+
+        hidden[...] = stream[...] + nn(att[...], w[3 * D :, :])
         gain_out = dec_gains[1:2, :]
 
-        def out_norm(i):
-            rows = span(i, 48)
+        def head_both(i):
+            rows = span(i, L)
             out_b[rows, :] = norm_rows(hidden[rows, :], gain_out).astype(B16)
-
-        loop(8, out_norm)
-
-        def pixel_head(i):
-            rows = span(i, L)
             pred = nn(out_b[rows, :], head[...]) + head_bias[...]
             err[rows, :] = (pred - wanted[rows, :].astype(F32)).astype(B16)
-
-        loop(2, pixel_head)
-
-        def head_back(i):
-            rows = span(i, 96)
-            d_out = nt(err[rows, :], head[...])
-            value = norm_rows_back(hidden[rows, :], gain_out, d_out)
+            value = norm_rows_back(hidden[rows, :], gain_out, nt(err[rows, :], head[...]))
             d_hidden[rows, :] = value
             back[3, rows, :] = value.astype(B16)
 
-        loop(4, head_back)
-
-        def att_back(i):
-            cols = span(i, 256)
-            d_att[:, cols] = nt(back[3], w[pl.ds(pl.multiple_of(3 * D + i * 256, 256), 256), :]).astype(B16)
-
-        loop(4, att_back)
+        loop(2, head_both, 2)
+        d_att[...] = nt(back[3], w[3 * D :, :]).astype(B16)
 
         def attend_back(i):
             rows = span(i // 4, L)
@@ -339,16 +300,13 @@
             back[0, rows, cols] = fold_heads(nn(d_s, k[rows, cols])).astype(B16)
             back[1, rows, cols] = tn(d_s, stack_heads(q[rows, cols])).astype(B16)
 
-        loop(8, attend_back)
-
-        def act_back(i):
-            cols = span(i, 256)
-            total = nt(back[0], w[pl.ds(pl.multiple_of(i * 256, 256), 256), :])
-            total = total + nt(back[1], w[pl.ds(pl.multiple_of(D + i * 256, 256), 256), :])
-            total = total + nt(back[2], w[pl.ds(pl.multiple_of(2 * D + i * 256, 256), 256), :])
-            d_stream[:, cols] = total
-
-        loop(4, act_back)
+        loop(8, attend_back, 8)
+
+        for i in range(2):
+            cols = slice(i * 512, (i + 1) * 512)
+            total = nt(back[0], w[i * 512 : (i + 1) * 512, :])
+            total = total + nt(back[1], w[D + i * 512 : D + (i + 1) * 512, :])
+            d_stream[:, cols] = total + nt(back[2], w[2 * D + i * 512 : 2 * D + (i + 1) * 512, :])
 
         def stream_back(i):
             rows = span(i, 48)
@@ -360,7 +318,7 @@
             def _():
                 dlat[span(i // 4, VIS), :] = value.astype(B16)
 
-        loop(8, stream_back)
+        loop(8, stream_back, 4)
         dlat_copy.start()
         at[0] = act[...].T
         at[1] = att[...].T
@@ -370,7 +328,7 @@
             value = nn(at[blk // 3, span(i % 4, 256), :], back[blk])
             term[i // 4, (i // 2) % 2, i % 2] = value.astype(B16).reshape(4, 64, D)
 
-        loop(16, terms)
+        loop(16, terms, 4)
         for s in range(2):
             for j in range(4):
                 for t in range(8):
@@ -387,7 +345,7 @@
             value = nn(normed_t[span(i, 256), :], dlat_in[...])
             term[i // 4, (i // 2) % 2, i % 2] = value.astype(B16).reshape(4, 64, D)
 
-        loop(16, terms)
+        loop(16, terms, 8)
 
     def send(src, dst, send_s, recv_s, who):
         copy = remote(src, dst, send_s, recv_s, who)
@@ -442,7 +400,7 @@
             d_norm[:, cols] = scaled
             return inner + jnp.sum(scaled * xb[:, cols].astype(F32), axis=-1, keepdims=True)
 
-        inner = lax.fori_loop(0, 16, step, acc2) * (1.0 / DE)
+        inner = lax.fori_loop(0, 16, step, acc2, unroll=4) * (1.0 / DE)
         rs = rstd[:, 0:1]
         factor = rs * rs * rs * inner
         for i in range(8):
@@ -511,7 +469,8 @@
             V((2 * VIS, DE), B16), V((2 * VIS, DE), B16), V((DE, 2 * VIS), B16), V((2 * VIS, 128), F32),
             V((2 * VIS, D), F32), V((2 * VIS, DE), F32),
             V((ROWS, D), F32), V((ROWS, D), F32), V((ROWS, D), F32), V((ROWS, D), F32), V((8, ROWS, 128), F32),
-            V((ROWS, D), B16), V((ROWS, D), B16), V((ROWS, D), B16), V((ROWS, D), B16), V((ROWS, D), B16),
+            V((ROWS, D), B16), V((ROWS - 2 * VIS, D), B16), V((2 * VIS, D), B16),
+            V((ROWS, D), B16), V((ROWS, D), B16), V((ROWS, D), B16), V((ROWS, D), B16),
             V((ROWS, D), B16), V((ROWS, D), B16), V((4, ROWS, D), B16), V((2, D, ROWS), B16),
             V((8, HEADS * L, L), F32), V((ROWS, 256), B16), V((ROWS, 256), B16), V((2, VIS, DE), B16),
             V((4, 2, 2, 4, 64, D), B16),

time: 93.8 us -> 79.8 us (0.85)
  the two profiles are of different devices: /device:TPU:0 before, /device:TPU:1 now
where the time goes in v2:
time: 79.8 us; the launch traced here: 79.6 us
  Pallas kernels  75.2 us (94%)
  local copies, waits for them, and re-layouts  3.73 us (5%)
    pallas_call x1, Pallas kernels, on_device(): pl.pallas_call(functools.partial(kernel, 1.0 / count), out_shape=(jax.Sha...  75.2 us
    unnamed x2, local copies, waits for them, and re-layouts  3.73 us

profile of v2, /device:TPU:1, one launch (start us, length us, event | category | flops | bytes accessed | tf_op | source)
XLA Modules:
  0.0 79.6 jit_solution(12571196477873357163)
XLA Ops:
  0.6 75.2 %window.1 = (bf16[2,48,4096]{2,1,0:T(8,128)(2,1)}, f32[64,1024]{1,0:T(8,128)}) custom-call(bf16[96,4096]{1,0:T(8,128)(2,1)} %bitcast.12, bf16[4096,1024]{1,0:T(8,128)(2,1)} %bitcast.11, f32[1,4096]{1,0:T(1,128)} %bitcast.16, f32[1,1024]{1,0:T(1,128)} %bitcast.17, f32[1,1024]{1,0:T(1,128)} %bitcast.18, f32[192,1024]{1,0:T(8,128)} %pos_hbm.1, ...), custom_call_target="tpu_custom_call" | custom-call | tf_op jit(solution)/shard_map/window/pallas_call | solution.py:461
  75.8 2.1 %copy.16 = bf16[1,2,1,48,4096]{4,3,2,1,0:T(8,128)(2,1)} copy(bf16[1,2,1,48,4096]{4,3,2,1,0:T(8,128)(2,1)} %bitcast.13) | data formatting | bytes 1572864
  77.9 1.7 %copy.17 = f32[1,64,1024]{2,1,0:T(8,128)} copy(f32[1,64,1024]{2,1,0:T(8,128)} %bitcast.14) | data formatting | bytes 524288

commit v3 on v2

--- a/solution.py
+++ b/solution.py
@@ -76,51 +76,72 @@
     return rstd * scaled - values * (rstd * rstd * rstd) * inner
 
 
-class Ax:
-    def __init__(self, view, r1, r2, ss, rs, plus, minus, send):
-        self.view, self.r1, self.r2 = view, r1, r2
-        self.ss, self.rs, self.plus, self.minus, self.send = ss, rs, plus, minus, send
+class Chunk:
+    def __init__(self, view, pick, r1, r2, acc, r3, sems, first, second, send):
+        self.view, self.pick, self.r1, self.r2, self.acc, self.r3 = view, pick, r1, r2, acc, r3
+        self.s1, self.v1, self.s2, self.v2 = sems
+        self.first, self.second, self.send = first, second, send
 
     def half(self, ref, h):
         n = ref.shape[0] // 2
         return ref.at[pl.ds(h * n, n)]
 
     def go(self, src, dst, k, who):
-        return self.send(src, dst, self.ss.at[k], self.rs.at[k], who)
+        return self.send(src, dst, self.s1.at[k], self.v1.at[k], who)
 
     def step1(self):
-        self.c0 = self.go(self.half(self.view(0), 0), self.r1.at[0], 0, self.plus)
-        self.c1 = self.go(self.half(self.view(0), 1), self.r1.at[1], 1, self.minus)
+        plus, minus = self.first[1:3]
+        self.c0 = self.go(self.half(self.view(0), 0), self.r1.at[0], 0, plus)
+        self.c1 = self.go(self.half(self.view(0), 1), self.r1.at[1], 1, minus)
 
     def step2(self):
-        self.c2 = self.go(self.half(self.view(1), 1), self.half(self.r2.at[0], 1), 2, self.plus)
-        self.c3 = self.go(self.half(self.view(2), 0), self.half(self.r2.at[1], 0), 3, self.minus)
+        plus, minus = self.first[1:3]
+        self.c2 = self.go(self.half(self.view(1), 1), self.half(self.r2.at[0], 1), 2, plus)
+        self.c3 = self.go(self.half(self.view(2), 0), self.half(self.r2.at[1], 0), 3, minus)
 
     def step3(self):
+        plus, minus = self.first[1:3]
         self.c0.wait_recv()
         mine = self.half(self.view(1), 0)
         mine[...] = mine[...] + self.r1[0]
-        self.c4 = self.go(mine, self.half(self.r2.at[0], 0), 4, self.plus)
+        self.c4 = self.go(mine, self.half(self.r2.at[0], 0), 4, plus)
         self.c1.wait_recv()
         mine = self.half(self.view(2), 1)
         mine[...] = mine[...] + self.r1[1]
-        self.c5 = self.go(mine, self.half(self.r2.at[1], 1), 5, self.minus)
-
-    def finish_waits(self):
+        self.c5 = self.go(mine, self.half(self.r2.at[1], 1), 5, minus)
+
+    def step4(self):
         for copy in (self.c2, self.c3, self.c4, self.c5):
             copy.wait_recv()
+        self.direct = []
+        for j in range(4):
+            value = self.pick(self.view(3), j).astype(F32)
+            value = value + self.pick(self.r2.at[0], j).astype(F32) + self.pick(self.r2.at[1], j).astype(F32)
+            self.acc[j] = value.astype(B16)
+            if j < 3:
+                self.direct.append(
+                    self.send(self.acc.at[j], self.r3.at[j], self.s2.at[j], self.v2.at[j], self.second[j])
+                )
+
+    def step5(self):
+        value = self.acc[3].astype(F32)
+        for j in range(3):
+            self.direct[j].wait_recv()
+            value = value + self.r3[j].astype(F32)
+        return value
 
 
 def kernel(
     scale,
     x_hbm, w_hbm, enc_gain, enc_bias, mask_token, pos_hbm, dec_gains, head_hbm, head_bias, order, tgt_hbm,
     g_out, w_out,
-    w, pos, head, tgt, lat, lat_in, dlat, dlat_in,
-    xb, normed, normed_t, rstd, acc, d_norm,
+    w, pos, head, tgt, lat, lat_in, dlat, dl_all,
+    xb, pack, nq, rstd, acc, d_norm,
     stream, hidden, d_hidden, d_stream, tall, act, act_m, act_v, q, k, v, att, out_b, d_att, back, at, probs, wanted, err, gbuf,
-    term, core_x, core_y, r1_x, r1_y, r2_x, r2_y, acc2_x, acc2_y, s1_x, s1_y, s2_x, s2_y, zr,
-    w_sem, in_sem, out_sem, grp_send, grp_recv,
-    core_send, core_recv, ssem, rsem, ssem2, rsem2, zsend, zrecv,
+    term, core_x, core_y, d1x, d1y, d2x, d2y, d3x, d3y, d4x, d4y, zr,
+    term_e, e1, e2, e3, e4,
+    w_sem, in_sem, out_sem, lat_send, lat_recv, dl_send, dl_recv, fw_send, fw_recv, nq_send, nq_recv,
+    core_send, core_recv, s1, v1, s2, v2, zsend, zrecv,
 ):
     dp = lax.axis_index("dp")
     x = lax.axis_index("section")
@@ -138,11 +159,15 @@
     to_core = {"dp": y * 4 + z * 2 + (1 - c)}
     to_z = {"dp": y * 4 + (1 - z) * 2 + c}
     to_grp = {"grp": 1 - grp}
+    to_cross = {"grp": 1 - grp, "dp": y * 4 + (1 - z) * 2 + c}
+    to_diag = {"dp": y * 4 + (1 - z) * 2 + (1 - c)}
     xs = [(x + 2) % 4, (x + 1) % 4, (x + 3) % 4, x]
     ys = [(y + 2) % 4, (y + 1) % 4, (y + 3) % 4, y]
 
     barrier = pltpu.get_barrier_semaphore()
-    for who in (to_grp, to_core, to_z, at_x(xs[1]), at_x(xs[2]), at_y(ys[1]), at_y(ys[2])):
+    to_x = [at_x(xs[j]) for j in range(3)]
+    to_y = [at_y(ys[j]) for j in range(3)]
+    for who in [to_grp, to_cross, to_core, to_z, to_diag] + to_x + to_y:
         pl.semaphore_signal(barrier, inc=1, device_id=who, device_id_type=MESH)
 
     def remote(src, dst, send, recv, who):
@@ -150,6 +175,15 @@
             src_ref=src, dst_ref=dst, send_sem=send, recv_sem=recv, device_id=who, device_id_type=MESH
         )
 
+    def sender(started):
+        def send(src, dst, send_s, recv_s, who):
+            copy = remote(src, dst, send_s, recv_s, who)
+            copy.start()
+            started.append(copy)
+            return copy
+
+        return send
+
     def w_copy(i):
         rows = pl.ds(pl.multiple_of(i * 512, 512), 512)
         return pltpu.make_async_copy(w_hbm.at[rows], w.at[rows], w_sem.at[i])
@@ -158,8 +192,7 @@
     pos_copy = pltpu.make_async_copy(pos_hbm, pos, in_sem.at[1])
     head_copy = pltpu.make_async_copy(head_hbm, head, in_sem.at[2])
     tgt_copy = pltpu.make_async_copy(tgt_hbm, tgt, in_sem.at[3])
-    lat_copy = remote(lat, lat_in, grp_send.at[0], grp_recv.at[0], to_grp)
-    dlat_copy = remote(dlat, dlat_in, grp_send.at[1], grp_recv.at[1], to_grp)
+    lat_copy = remote(lat, lat_in, lat_send.at[0], lat_recv.at[0], to_grp)
     g_copy = pltpu.make_async_copy(gbuf, g_out, out_sem.at[0])
 
     @pl.when(grp == 0)
@@ -188,7 +221,8 @@
             cols = span(i, 512)
             block = xb[:, cols].astype(F32) * rstd[:, 0:1] * enc_gain[:, cols]
             block = block.astype(B16)
-            normed[:, cols] = block
+            for j in range(2):
+                pack[(i % 2) * 2 + j, :, span(i // 2, 256)] = block[:, j * 256 : (j + 1) * 256]
             w_copy(i).wait()
             acc[...] += nn(block, w[cols, :])
 
@@ -231,18 +265,21 @@
             w_copy(i).wait()
         head_copy.wait()
 
-    pl.semaphore_wait(barrier, 7)
+    pl.semaphore_wait(barrier, 11)
 
     @pl.when(grp == 0)
     def _():
         lat_copy.start()
-
-        def flip(i):
-            cols = span(i, 512)
-            normed_t[cols, :] = normed[:, cols].T
-
-        loop(8, flip, 4)
         lat_copy.wait_send()
+        me = z * 2 + c
+        nq[me] = pack[me]
+        copies = []
+        for j, (place, who) in enumerate(((z * 2 + 1 - c, to_core), ((1 - z) * 2 + c, to_z), ((1 - z) * 2 + 1 - c, to_diag))):
+            copies.append(remote(pack.at[place], nq.at[me], nq_send.at[j], nq_recv.at[j], who))
+            copies[-1].start()
+        for copy in copies:
+            copy.wait()
+        at[0] = nq[...].reshape(4 * 2 * VIS, D).T
 
     @pl.when(grp == 1)
     def _():
@@ -302,152 +339,188 @@
 
         loop(8, attend_back, 8)
 
-        for i in range(2):
-            cols = slice(i * 512, (i + 1) * 512)
-            total = nt(back[0], w[i * 512 : (i + 1) * 512, :])
-            total = total + nt(back[1], w[D + i * 512 : D + (i + 1) * 512, :])
-            d_stream[:, cols] = total + nt(back[2], w[2 * D + i * 512 : 2 * D + (i + 1) * 512, :])
-
-        def stream_back(i):
-            rows = span(i, 48)
-            value = d_hidden[rows, :] + norm_rows_back(stream[rows, :], gain, d_stream[rows, :])
+        def act_back(part_of):
+            total = nt(part_of(0), w[:D, :])
+            total = total + nt(part_of(1), w[D : 2 * D, :])
+            return total + nt(part_of(2), w[2 * D : 3 * D, :])
+
+        def both(ref):
+            return jnp.concatenate([ref[:VIS, :], ref[L : L + VIS, :]], 0)
+
+        def keep(start, value):
+            rows = value.shape[0]
             for t in range(8):
-                tall[t, rows, :] = value[:, t * 128 : (t + 1) * 128]
-
-            @pl.when(i % 4 == 0)
-            def _():
-                dlat[span(i // 4, VIS), :] = value.astype(B16)
-
-        loop(8, stream_back, 4)
-        dlat_copy.start()
+                tall[t, start : start + rows, :] = value[:, t * 128 : (t + 1) * 128]
+
+        upstream = act_back(lambda part: both(back.at[part]))
+        for s in range(2):
+            rows = slice(s * L, s * L + VIS)
+            value = d_hidden[rows, :] + norm_rows_back(stream[rows, :], gain, upstream[s * VIS : (s + 1) * VIS])
+            keep(s * L, value)
+            dlat[s * VIS : (s + 1) * VIS, :] = value.astype(B16)
+        slot = dl_all.at[z * 2 + c]
+        d_copies = [
+            remote(dlat, slot, dl_send.at[0], dl_recv.at[z], to_grp),
+            remote(dlat, slot, dl_send.at[1], dl_recv.at[z], to_cross),
+        ]
+        for copy in d_copies:
+            copy.start()
         at[0] = act[...].T
         at[1] = att[...].T
 
-        def terms(i):
-            blk = i // 4
-            value = nn(at[blk // 3, span(i % 4, 256), :], back[blk])
-            term[i // 4, (i // 2) % 2, i % 2] = value.astype(B16).reshape(4, 64, D)
-
-        loop(16, terms, 4)
-        for s in range(2):
-            for j in range(4):
-                for t in range(8):
-                    start = j * D + t * 128
-                    gbuf[s, :, start : start + 128] = tall[t, pl.ds(s * L + j, VIS, stride=4), :].astype(B16)
-        g_copy.start()
-        dlat_copy.wait_send()
+        def masked_rows():
+            for s in range(2):
+                d_stream[s * L + VIS : (s + 1) * L, :] = act_back(lambda part: back[part, s * L + VIS : (s + 1) * L, :])
+                for i in range(1, 4):
+                    rows = slice(s * L + i * VIS, s * L + (i + 1) * VIS)
+                    value = d_hidden[rows, :] + norm_rows_back(stream[rows, :], gain, d_stream[rows, :])
+                    keep(s * L + i * VIS, value)
+            for s in range(2):
+                for j in range(4):
+                    for t in range(8):
+                        start = j * D + t * 128
+                        gbuf[s, :, start : start + 128] = tall[t, pl.ds(s * L + j, VIS, stride=4), :].astype(B16)
+            g_copy.start()
+
+        started = []
+        send = sender(started)
+
+        def px(g, core, j):
+            return term.at[g, :, :, core, j, pl.ds(0, 32)]
+
+        def py(g, core, j):
+            return term.at[g, j, :, core, :, pl.ds(32, 32)]
+
+        def make(g):
+            sems = lambda a: (s1.at[g, a], v1.at[g, a], s2.at[g, a], v2.at[g, a])
+            return (
+                Chunk(
+                    lambda j: px(g, c, xs[j]), lambda ref, j: ref[ys[j]],
+                    d1x.at[g], d2x.at[g], d3x.at[g], d4x.at[g], sems(0), to_x, to_y, send,
+                ),
+                Chunk(
+                    lambda j: py(g, c, ys[j]), lambda ref, j: ref[:, xs[j]],
+                    d1y.at[g], d2y.at[g], d3y.at[g], d4y.at[g], sems(1), to_y, to_x, send,
+                ),
+            )
+
+        chunks = [make(g) for g in range(4)]
+        cores, zs = {}, {}
+
+        def stage(k, g):
+            if k == 0:
+                for blk in range(4):
+                    value = nn(at[blk // 3], back[blk, :, g * 256 : (g + 1) * 256])
+                    term[g, blk] = value.astype(B16).reshape(2, 2, 4, 64, 256)
+                whole = term.at[g, :, :, 1 - c]
+                cores[g, 0] = send(
+                    whole.at[:, :, :, pl.ds(0, 32)], core_x.at[g], core_send.at[g, 0], core_recv.at[g, 0], to_core
+                )
+                cores[g, 1] = send(
+                    whole.at[:, :, :, pl.ds(32, 32)], core_y.at[g], core_send.at[g, 1], core_recv.at[g, 1], to_core
+                )
+            if k == 1:
+                for a in range(2):
+                    cores[g, a].wait_recv()
+                    got = (core_x, core_y)[a].at[g]
+                    for j in range(4):
+                        mine = chunks[g][a].view(j)
+                        extra = got[:, :, xs[j]] if a == 0 else got[ys[j]]
+                        mine[...] = mine[...] + extra
+                        if j == 0:
+                            chunks[g][a].step1()
+                        if j == 2:
+                            chunks[g][a].step2()
+            if k == 2:
+                for a in range(2):
+                    chunks[g][a].step3()
+            if k == 3:
+                for a in range(2):
+                    chunks[g][a].step4()
+            if k == 4:
+                for a in range(2):
+                    value = chunks[g][a].step5()
+                    mine = chunks[g][a].acc.at[3]
+                    mine[...] = value.astype(B16)
+                    zs[g, a] = send(mine.at[1 - z], zr.at[g, a], zsend.at[g, a], zrecv.at[g, a], to_z)
+            if k == 5:
+                for a in range(2):
+                    zs[g, a].wait_recv()
+                    value = chunks[g][a].acc[3, z].astype(F32) + zr[g, a].astype(F32)
+                    w_out[a * 32 : (a + 1) * 32, g * 256 : (g + 1) * 256] = value * scale
+
+        for d in range(9):
+            for g in range(4):
+                if 0 <= d - g < 6:
+                    stage(d - g, g)
+            if d == 4:
+                masked_rows()
+        for copy in d_copies + started:
+            copy.wait_send()
 
     @pl.when(grp == 0)
     def _():
-        dlat_copy.wait_recv()
-
-        def terms(i):
-            value = nn(normed_t[span(i, 256), :], dlat_in[...])
-            term[i // 4, (i // 2) % 2, i % 2] = value.astype(B16).reshape(4, 64, D)
-
-        loop(16, terms, 8)
-
-    def send(src, dst, send_s, recv_s, who):
-        copy = remote(src, dst, send_s, recv_s, who)
-        copy.start()
-        started.append(copy)
-        return copy
-
-    started = []
-
-    def px(j, core):
-        return term.at[:, :, core, xs[j], pl.ds(0, 32)]
-
-    def py(j, core):
-        return term.at[ys[j], :, core, :, pl.ds(32, 32)]
-
-    parts = (px, py)
-    corebufs = (core_x, core_y)
-    cores = {}
-    for a, j in ((0, 0), (1, 0), (0, 1), (0, 2), (1, 1), (1, 2), (0, 3), (1, 3)):
-        cores[a, j] = send(
-            parts[a](j, 1 - c), corebufs[a].at[j], core_send.at[a, j], core_recv.at[a, j], to_core
-        )
-
-    def merge(a, j):
-        cores[a, j].wait_recv()
-        mine = parts[a](j, c)
-        mine[...] = mine[...] + corebufs[a][j]
-
-    first = (
-        Ax(lambda j: px(j, c), r1_x, r2_x, ssem.at[0], rsem.at[0], at_x(xs[1]), at_x(xs[2]), send),
-        Ax(lambda j: py(j, c), r1_y, r2_y, ssem.at[1], rsem.at[1], at_y(ys[1]), at_y(ys[2]), send),
-    )
-    second = (
-        Ax(lambda j: acc2_x.at[j], s1_x, s2_x, ssem2.at[0], rsem2.at[0], at_y(ys[1]), at_y(ys[2]), send),
-        Ax(lambda j: acc2_y.at[j], s1_y, s2_y, ssem2.at[1], rsem2.at[1], at_x(xs[1]), at_x(xs[2]), send),
-    )
-    for a in (0, 1):
-        merge(a, 0)
-        first[a].step1()
-    for a in (0, 1):
-        merge(a, 1)
-        merge(a, 2)
-        first[a].step2()
-    @pl.when(grp == 0)
-    def _():
-        acc2 = jnp.zeros((2 * VIS, 1), F32)
-
-        def step(i, inner):
-            cols = span(i, 256)
-            d_n = nt(dlat_in[...], w[cols, :])
-            scaled = d_n * enc_gain[:, cols]
+        passed = []
+        for zz in range(2):
+            slot = dl_all.at[zz * 2 + c]
+            remote(dlat, slot, dl_send.at[0], dl_recv.at[zz], to_grp).wait_recv()
+            passed.append(remote(slot, slot, fw_send.at[zz], fw_recv.at[zz], to_core))
+            passed[-1].start()
+        for copy in passed:
+            copy.wait_recv()
+        started = []
+        send = sender(started)
+
+        def make(g):
+            sems = lambda a: (s1.at[g, a], v1.at[g, a], s2.at[g, a], v2.at[g, a])
+            return (
+                Chunk(
+                    lambda j: term_e.at[g, :, xs[j], pl.ds(0, 32)], lambda ref, j: ref[ys[j]],
+                    e1.at[g, 0], e2.at[g, 0], e3.at[g, 0], e4.at[g, 0], sems(0), to_x, to_y, send,
+                ),
+                Chunk(
+                    lambda j: term_e.at[g, ys[j], :, pl.ds(32, 32)], lambda ref, j: ref[xs[j]],
+                    e1.at[g, 1], e2.at[g, 1], e3.at[g, 1], e4.at[g, 1], sems(1), to_y, to_x, send,
+                ),
+            )
+
+        chunks = [make(g) for g in range(2)]
+        for g in range(2):
+            every = dl_all[:, :, g * 512 : (g + 1) * 512].reshape(4 * 2 * VIS, 512)
+            term_e[g] = nn(at[0], every).astype(B16).reshape(4, 4, 64, 512)
+            for a in range(2):
+                chunks[g][a].step1()
+                chunks[g][a].step2()
+
+        own = dl_all[z * 2 + c]
+        inner = jnp.zeros((2 * VIS, 1), F32)
+        for i in range(4):
+            cols = slice(i * D, (i + 1) * D)
+            scaled = nt(own, w[cols, :]) * enc_gain[:, cols]
             d_norm[:, cols] = scaled
-            return inner + jnp.sum(scaled * xb[:, cols].astype(F32), axis=-1, keepdims=True)
-
-        inner = lax.fori_loop(0, 16, step, acc2, unroll=4) * (1.0 / DE)
+            inner = inner + jnp.sum(scaled * xb[:, cols].astype(F32), axis=-1, keepdims=True)
+            if i == 1:
+                for g in range(2):
+                    for a in range(2):
+                        chunks[g][a].step3()
         rs = rstd[:, 0:1]
-        factor = rs * rs * rs * inner
+        factor = rs * rs * rs * (inner * (1.0 / DE))
+        for g in range(2):
+            for a in range(2):
+                chunks[g][a].step4()
         for i in range(8):
             cols = slice(i * 512, (i + 1) * 512)
             value = (rs * d_norm[:, cols] - xb[:, cols].astype(F32) * factor).astype(B16)
             gbuf[0, :, cols] = value[:VIS]
             gbuf[1, :, cols] = value[VIS:]
         g_copy.start()
-
-    for a in (0, 1):
-        first[a].step3()
-    for a in (0, 1):
-        merge(a, 3)
-
-    def total(a, j):
-        ax = first[a]
-        if a == 0:
-            rows = lambda ref: ref[ys[j]]
-        else:
-            rows = lambda ref: ref[:, xs[j]]
-        value = rows(ax.view(3)).astype(F32) + rows(ax.r2.at[0]).astype(F32) + rows(ax.r2.at[1]).astype(F32)
-        second[a].view(j)[...] = value.astype(B16)
-
-    for a in (0, 1):
-        first[a].finish_waits()
-        total(a, 0)
-        second[a].step1()
-        total(a, 1)
-        total(a, 2)
-        second[a].step2()
-        total(a, 3)
-    for a in (0, 1):
-        second[a].step3()
-    zcopies = []
-    for a in (0, 1):
-        ax = second[a]
-        ax.finish_waits()
-        mine = ax.view(3)
-        value = mine[...].astype(F32) + ax.r2[0].astype(F32) + ax.r2[1].astype(F32)
-        mine[...] = value.astype(B16)
-        zcopies.append(send(mine.at[1 - z], zr.at[a], zsend.at[a], zrecv.at[a], to_z))
-    for a in (0, 1):
-        zcopies[a].wait_recv()
-        w_out[a * 32 : (a + 1) * 32, :] = (second[a].view(3)[z].astype(F32) + zr[a].astype(F32)) * scale
+        for g in range(2):
+            for a in range(2):
+                w_out[a * 32 : (a + 1) * 32, g * 512 : (g + 1) * 512] = chunks[g][a].step5() * scale
+        for copy in passed + started:
+            copy.wait_send()
+
     g_copy.wait()
-    for copy in started:
-        copy.wait_send()
 
 
 def on_device(
@@ -465,24 +538,25 @@
         out_specs=(hbm, full),
         scratch_shapes=[
             V((DE, D), B16), V((L, D), F32), V((D, 256), B16), V((2, L, 256), B16),
-            V((2 * VIS, D), B16), V((2 * VIS, D), B16), V((2 * VIS, D), B16), V((2 * VIS, D), B16),
-            V((2 * VIS, DE), B16), V((2 * VIS, DE), B16), V((DE, 2 * VIS), B16), V((2 * VIS, 128), F32),
+            V((2 * VIS, D), B16), V((2 * VIS, D), B16), V((2 * VIS, D), B16), V((4, 2 * VIS, D), B16),
+            V((2 * VIS, DE), B16), V((4, 2 * VIS, D), B16), V((4, 2 * VIS, D), B16), V((2 * VIS, 128), F32),
             V((2 * VIS, D), F32), V((2 * VIS, DE), F32),
             V((ROWS, D), F32), V((ROWS, D), F32), V((ROWS, D), F32), V((ROWS, D), F32), V((8, ROWS, 128), F32),
             V((ROWS, D), B16), V((ROWS - 2 * VIS, D), B16), V((2 * VIS, D), B16),
             V((ROWS, D), B16), V((ROWS, D), B16), V((ROWS, D), B16), V((ROWS, D), B16),
             V((ROWS, D), B16), V((ROWS, D), B16), V((4, ROWS, D), B16), V((2, D, ROWS), B16),
             V((8, HEADS * L, L), F32), V((ROWS, 256), B16), V((ROWS, 256), B16), V((2, VIS, DE), B16),
-            V((4, 2, 2, 4, 64, D), B16),
-            V((4, 4, 2, 32, D), B16), V((4, 2, 4, 32, D), B16),
-            V((2, 2, 2, 32, D), B16), V((2, 1, 4, 32, D), B16),
-            V((2, 4, 2, 32, D), B16), V((2, 2, 4, 32, D), B16),
-            V((4, 2, 32, D), B16), V((4, 2, 32, D), B16),
-            V((2, 1, 32, D), B16), V((2, 1, 32, D), B16),
-            V((2, 2, 32, D), B16), V((2, 2, 32, D), B16),
-            V((2, 32, D), B16),
-            S((8,)), S((4,)), S((1,)), S((2,)), S((2,)),
-            S((2, 4)), S((2, 4)), S((2, 6)), S((2, 6)), S((2, 6)), S((2, 6)), S((2,)), S((2,)),
+            V((4, 4, 2, 2, 4, 64, 256), B16),
+            V((4, 4, 2, 4, 32, 256), B16), V((4, 4, 2, 4, 32, 256), B16),
+            V((4, 2, 2, 2, 32, 256), B16), V((4, 2, 1, 4, 32, 256), B16),
+            V((4, 2, 4, 2, 32, 256), B16), V((4, 2, 2, 4, 32, 256), B16),
+            V((4, 4, 2, 32, 256), B16), V((4, 4, 2, 32, 256), B16),
+            V((4, 3, 2, 32, 256), B16), V((4, 3, 2, 32, 256), B16),
+            V((4, 2, 32, 256), B16),
+            V((2, 4, 4, 64, 512), B16), V((2, 2, 2, 2, 32, 512), B16), V((2, 2, 2, 4, 32, 512), B16),
+            V((2, 2, 4, 32, 512), B16), V((2, 2, 3, 32, 512), B16),
+            S((8,)), S((4,)), S((1,)), S((1,)), S((1,)), S((2,)), S((2,)), S((2,)), S((2,)), S((3,)), S((3,)),
+            S((4, 2)), S((4, 2)), S((4, 2, 6)), S((4, 2, 6)), S((4, 2, 3)), S((4, 2, 3)), S((4, 2)), S((4, 2)),
         ],
         compiler_params=pltpu.CompilerParams(
             collective_id=0, has_side_effects=True, vmem_limit_bytes=60 * 2**20

time: 79.8 us -> 72.2 us (0.905)
  the two profiles are of different devices: /device:TPU:1 before, /device:TPU:64 now
where the time goes in v3:
time: 72.2 us; the launch traced here: 71.9 us
  Pallas kernels  67.6 us (94%)
  local copies, waits for them, and re-layouts  3.73 us (5%)
    pallas_call x1, Pallas kernels, on_device(): pl.pallas_call(functools.partial(kernel, 1.0 / count), out_shape=(jax.Sha...  67.6 us
    unnamed x2, local copies, waits for them, and re-layouts  3.73 us

profile of v3, /device:TPU:64, one launch (start us, length us, event | category | flops | bytes accessed | tf_op | source)
XLA Modules:
  0.0 71.9 jit_solution(11677028701470618879)
XLA Ops:
  0.6 67.6 %window.1 = (bf16[2,48,4096]{2,1,0:T(8,128)(2,1)}, f32[64,1024]{1,0:T(8,128)}) custom-call(bf16[96,4096]{1,0:T(8,128)(2,1)} %bitcast.12, bf16[4096,1024]{1,0:T(8,128)(2,1)} %bitcast.11, f32[1,4096]{1,0:T(1,128)} %bitcast.16, f32[1,1024]{1,0:T(1,128)} %bitcast.17, f32[1,1024]{1,0:T(1,128)} %bitcast.18, f32[192,1024]{1,0:T(8,128)} %pos_hbm.1, ...), custom_call_target="tpu_custom_call" | custom-call | tf_op jit(solution)/shard_map/window/pallas_call | solution.py:534
  68.2 2.1 %copy.16 = bf16[1,2,1,48,4096]{4,3,2,1,0:T(8,128)(2,1)} copy(bf16[1,2,1,48,4096]{4,3,2,1,0:T(8,128)(2,1)} %bitcast.13) | data formatting | bytes 1572864
  70.3 1.7 %copy.17 = f32[1,64,1024]{2,1,0:T(8,128)} copy(f32[1,64,1024]{2,1,0:T(8,128)} %bitcast.14) | data formatting | bytes 524288

commit v4 on v3

--- a/solution.py
+++ b/solution.py
@@ -12,6 +12,11 @@
 B16 = jnp.bfloat16
 F32 = jnp.float32
 EPS = 1e-06
+PLAN = (
+    "b0", "00", "b1", "b2", "10", "b3", "v", "01", "20", "02",
+    "11", "03", "12", "30", "13", "21", "m", "22", "31", "40",
+    "23", "32", "41", "50", "33", "42", "51", "43", "52", "53",
+)
 D = 1024
 DE = 4096
 L = 192
@@ -80,6 +85,8 @@
     def __init__(self, view, pick, r1, r2, acc, r3, sems, first, second, send):
         self.view, self.pick, self.r1, self.r2, self.acc, self.r3 = view, pick, r1, r2, acc, r3
         self.s1, self.v1, self.s2, self.v2 = sems
+        if isinstance(pick, tuple):
+            self.pick_z, self.targets = pick
         self.first, self.second, self.send = first, second, send
 
     def half(self, ref, h):
@@ -122,6 +129,34 @@
                 self.direct.append(
                     self.send(self.acc.at[j], self.r3.at[j], self.s2.at[j], self.v2.at[j], self.second[j])
                 )
+
+    def cross(self, send_sem, recv_sem, to_z, z, zr):
+        for copy in (self.c2, self.c3, self.c4, self.c5):
+            copy.wait_recv()
+        for j, zz in ((0, 1 - z), (1, z)):
+            value = self.pick_z(self.view(3), zz).astype(F32)
+            value = value + self.pick_z(self.r2.at[0], zz).astype(F32) + self.pick_z(self.r2.at[1], zz).astype(F32)
+            self.acc[j] = value.astype(B16)
+            if j == 0:
+                self.zc = self.send(self.acc.at[0], zr, send_sem, recv_sem, to_z)
+
+    def spread(self, zr):
+        self.zc.wait_recv()
+        self.direct = []
+        self.acc[1] = self.acc[1] + zr[...]
+        for j in range(3):
+            self.direct.append(
+                self.send(
+                    self.acc.at[1, self.targets[j]], self.r3.at[j], self.s2.at[j], self.v2.at[j], self.second[j]
+                )
+            )
+
+    def last(self):
+        value = self.acc[1, self.targets[3]].astype(F32)
+        for j in range(3):
+            self.direct[j].wait_recv()
+            value = value + self.r3[j].astype(F32)
+        return value
 
     def step5(self):
         value = self.acc[3].astype(F32)
@@ -325,19 +360,21 @@
         loop(2, head_both, 2)
         d_att[...] = nt(back[3], w[3 * D :, :]).astype(B16)
 
-        def attend_back(i):
-            rows = span(i // 4, L)
-            cols = span(i % 4, GROUP)
-            p = probs[i]
-            up = stack_heads(d_att[rows, cols])
-            d_p = nt(up, v[rows, cols])
-            d_s = p * (d_p - jnp.sum(d_p * p, axis=-1, keepdims=True)) * shrink
-            d_s = d_s.astype(B16)
-            back[2, rows, cols] = tn(p.astype(B16), up).astype(B16)
-            back[0, rows, cols] = fold_heads(nn(d_s, k[rows, cols])).astype(B16)
-            back[1, rows, cols] = tn(d_s, stack_heads(q[rows, cols])).astype(B16)
-
-        loop(8, attend_back, 8)
+        at[0] = act[...].T
+        at[1] = att[...].T
+
+        def attend_back(g):
+            cols = slice(g * GROUP, (g + 1) * GROUP)
+            for s in range(2):
+                rows = slice(s * L, (s + 1) * L)
+                p = probs[s * 4 + g]
+                up = stack_heads(d_att[rows, cols])
+                d_p = nt(up, v[rows, cols])
+                d_s = p * (d_p - jnp.sum(d_p * p, axis=-1, keepdims=True)) * shrink
+                d_s = d_s.astype(B16)
+                back[2, rows, cols] = tn(p.astype(B16), up).astype(B16)
+                back[0, rows, cols] = fold_heads(nn(d_s, k[rows, cols])).astype(B16)
+                back[1, rows, cols] = tn(d_s, stack_heads(q[rows, cols])).astype(B16)
 
         def act_back(part_of):
             total = nt(part_of(0), w[:D, :])
@@ -352,21 +389,21 @@
             for t in range(8):
                 tall[t, start : start + rows, :] = value[:, t * 128 : (t + 1) * 128]
 
-        upstream = act_back(lambda part: both(back.at[part]))
-        for s in range(2):
-            rows = slice(s * L, s * L + VIS)
-            value = d_hidden[rows, :] + norm_rows_back(stream[rows, :], gain, upstream[s * VIS : (s + 1) * VIS])
-            keep(s * L, value)
-            dlat[s * VIS : (s + 1) * VIS, :] = value.astype(B16)
-        slot = dl_all.at[z * 2 + c]
-        d_copies = [
-            remote(dlat, slot, dl_send.at[0], dl_recv.at[z], to_grp),
-            remote(dlat, slot, dl_send.at[1], dl_recv.at[z], to_cross),
-        ]
-        for copy in d_copies:
-            copy.start()
-        at[0] = act[...].T
-        at[1] = att[...].T
+        def visible_rows():
+            upstream = act_back(lambda part: both(back.at[part]))
+            for s in range(2):
+                rows = slice(s * L, s * L + VIS)
+                value = d_hidden[rows, :] + norm_rows_back(stream[rows, :], gain, upstream[s * VIS : (s + 1) * VIS])
+                keep(s * L, value)
+                dlat[s * VIS : (s + 1) * VIS, :] = value.astype(B16)
+            slot = dl_all.at[z * 2 + c]
+            d_copies = [
+                remote(dlat, slot, dl_send.at[0], dl_recv.at[z], to_grp),
+                remote(dlat, slot, dl_send.at[1], dl_recv.at[z], to_cross),
+            ]
+            for copy in d_copies:
+                copy.start()
+            return d_copies
 
         def masked_rows():
             for s in range(2):
@@ -395,17 +432,17 @@
             sems = lambda a: (s1.at[g, a], v1.at[g, a], s2.at[g, a], v2.at[g, a])
             return (
                 Chunk(
-                    lambda j: px(g, c, xs[j]), lambda ref, j: ref[ys[j]],
+                    lambda j: px(g, c, xs[j]), (lambda ref, zz: ref[:, zz], ys),
                     d1x.at[g], d2x.at[g], d3x.at[g], d4x.at[g], sems(0), to_x, to_y, send,
                 ),
                 Chunk(
-                    lambda j: py(g, c, ys[j]), lambda ref, j: ref[:, xs[j]],
+                    lambda j: py(g, c, ys[j]), (lambda ref, zz: ref[zz], xs),
                     d1y.at[g], d2y.at[g], d3y.at[g], d4y.at[g], sems(1), to_y, to_x, send,
                 ),
             )
 
         chunks = [make(g) for g in range(4)]
-        cores, zs = {}, {}
+        cores = {}
 
         def stage(k, g):
             if k == 0:
@@ -436,25 +473,24 @@
                     chunks[g][a].step3()
             if k == 3:
                 for a in range(2):
-                    chunks[g][a].step4()
+                    chunks[g][a].cross(zsend.at[g, a], zrecv.at[g, a], to_z, z, zr.at[g, a])
             if k == 4:
                 for a in range(2):
-                    value = chunks[g][a].step5()
-                    mine = chunks[g][a].acc.at[3]
-                    mine[...] = value.astype(B16)
-                    zs[g, a] = send(mine.at[1 - z], zr.at[g, a], zsend.at[g, a], zrecv.at[g, a], to_z)
+                    chunks[g][a].spread(zr.at[g, a])
             if k == 5:
                 for a in range(2):
-                    zs[g, a].wait_recv()
-                    value = chunks[g][a].acc[3, z].astype(F32) + zr[g, a].astype(F32)
-                    w_out[a * 32 : (a + 1) * 32, g * 256 : (g + 1) * 256] = value * scale
-
-        for d in range(9):
-            for g in range(4):
-                if 0 <= d - g < 6:
-                    stage(d - g, g)
-            if d == 4:
+                    w_out[a * 32 : (a + 1) * 32, g * 256 : (g + 1) * 256] = chunks[g][a].last() * scale
+
+        d_copies = []
+        for word in PLAN:
+            if word == "v":
+                d_copies = visible_rows()
+            elif word == "m":
                 masked_rows()
+            elif word[0] == "b":
+                attend_back(int(word[1]))
+            else:
+                stage(int(word[0]), int(word[1]))
         for copy in d_copies + started:
             copy.wait_send()
 
@@ -550,9 +586,9 @@
             V((4, 4, 2, 4, 32, 256), B16), V((4, 4, 2, 4, 32, 256), B16),
             V((4, 2, 2, 2, 32, 256), B16), V((4, 2, 1, 4, 32, 256), B16),
             V((4, 2, 4, 2, 32, 256), B16), V((4, 2, 2, 4, 32, 256), B16),
-            V((4, 4, 2, 32, 256), B16), V((4, 4, 2, 32, 256), B16),
-            V((4, 3, 2, 32, 256), B16), V((4, 3, 2, 32, 256), B16),
-            V((4, 2, 32, 256), B16),
+            V((4, 2, 4, 32, 256), B16), V((4, 2, 4, 32, 256), B16),
+            V((4, 3, 32, 256), B16), V((4, 3, 32, 256), B16),
+            V((4, 2, 4, 32, 256), B16),
             V((2, 4, 4, 64, 512), B16), V((2, 2, 2, 2, 32, 512), B16), V((2, 2, 2, 4, 32, 512), B16),
             V((2, 2, 4, 32, 512), B16), V((2, 2, 3, 32, 512), B16),
             S((8,)), S((4,)), S((1,)), S((1,)), S((1,)), S((2,)), S((2,)), S((2,)), S((2,)), S((3,)), S((3,)),
@@ -566,6 +602,28 @@
         enc_input.reshape(2 * VIS, DE), weights[0], enc_gain[None], enc_bias[None], mask_token[None], pos_embed,
         dec_gains, head_weight, head_bias[None], order, targets.reshape(2, L, 256),
     )
+
+    def deliver(a_in, b_in, a_out, b_out, a_mid, b_mid, sem):
+        steps = []
+        for i in range(2):
+            steps.append((a_in.at[i], a_mid.at[i], a_out.at[i], sem.at[i]))
+        steps.append((b_in, b_mid, b_out, sem.at[2]))
+        for src, mid, _, one in steps:
+            pltpu.make_async_copy(src, mid, one).start()
+        for src, mid, dst, one in steps:
+            pltpu.make_async_copy(src, mid, one).wait()
+            pltpu.make_async_copy(mid, dst, one).start()
+        for _, mid, dst, one in steps:
+            pltpu.make_async_copy(mid, dst, one).wait()
+
+    grads, w_grad = pl.pallas_call(
+        deliver,
+        out_shape=(jax.ShapeDtypeStruct((2, VIS, DE), B16), jax.ShapeDtypeStruct((64, D), F32)),
+        in_specs=[hbm, hbm],
+        out_specs=(hbm, hbm),
+        scratch_shapes=[V((2, VIS, DE), B16), V((64, D), F32), S((3,))],
+        name="deliver",
+    )(grads, w_grad)
     return grads[None, :, None], w_grad[None]
 
 

time: 72.2 us -> 66.8 us (0.925); the launches traced: 71.9 us -> 65.7 us
  local copies, waits for them, and re-layouts: 3.73 us -> 0 us
  Pallas kernels: 67.6 us -> 64.9 us
    pallas_call x1, Pallas kernels: 67.6 us -> 62.9 us  [on_device(): pl.pallas_call(functools.partial(kernel, 1.0 / count), out_shape=(jax.Sha...]
    unnamed x2 -> x0, local copies, waits for them, and re-layouts: 3.73 us -> none
    pallas_call x0 -> x1, Pallas kernels: none -> 1.98 us  [on_device(): pl.pallas_call(deliver, out_shape=(jax.ShapeDtypeStruct((2, VIS, DE), B16...]
where the time goes in v4:
time: 66.8 us; the launch traced here: 65.7 us
  Pallas kernels  64.9 us (97%)
  between operations  0.84 us (1%)
    pallas_call x1, Pallas kernels, on_device(): pl.pallas_call(functools.partial(kernel, 1.0 / count), out_shape=(jax.Sha...  62.9 us
    pallas_call x1, Pallas kernels, on_device(): pl.pallas_call(deliver, out_shape=(jax.ShapeDtypeStruct((2, VIS, DE), B16...  1.98 us

profile of v4, /device:TPU:64, one launch (start us, length us, event | category | flops | bytes accessed | tf_op | source)
XLA Modules:
  0.0 65.7 jit_solution(8472559011150305661)
XLA Ops:
  0.6 62.9 %window.1 = (bf16[2,48,4096]{2,1,0:T(8,128)(2,1)}, f32[64,1024]{1,0:T(8,128)}) custom-call(bf16[96,4096]{1,0:T(8,128)(2,1)} %bitcast.12, bf16[4096,1024]{1,0:T(8,128)(2,1)} %bitcast.11, f32[1,4096]{1,0:T(1,128)} %bitcast.14, f32[1,1024]{1,0:T(1,128)} %bitcast.15, f32[1,1024]{1,0:T(1,128)} %bitcast.16, f32[192,1024]{1,0:T(8,128)} %pos_hbm.1, ...), custom_call_target="tpu_custom_call" | custom-call | tf_op jit(solution)/shard_map/window/pallas_call | solution.py:570
  63.5 2.0 %deliver.1 = (bf16[2,48,4096]{2,1,0:T(8,128)(2,1)}, f32[64,1024]{1,0:T(8,128)}) custom-call(bf16[2,48,4096]{2,1,0:T(8,128)(2,1)} %get-tuple-element.6.a_in, f32[64,1024]{1,0:T(8,128)} %get-tuple-element.7.b_in), custom_call_target="tpu_custom_call" | custom-call | tf_op jit(solution)/shard_map/deliver/pallas_call | solution.py:619

commit v5 on v4

--- a/solution.py
+++ b/solution.py
@@ -13,7 +13,7 @@
 F32 = jnp.float32
 EPS = 1e-06
 PLAN = (
-    "b0", "00", "b1", "b2", "10", "b3", "v", "01", "20", "02",
+    "b0", "00", "b1", "b2", "b3", "10", "v", "01", "20", "02",
     "11", "03", "12", "30", "13", "21", "m", "22", "31", "40",
     "23", "32", "41", "50", "33", "42", "51", "43", "52", "53",
 )
@@ -168,13 +168,14 @@
 
 def kernel(
     scale,
-    x_hbm, w_hbm, enc_gain, enc_bias, mask_token, pos_hbm, dec_gains, head_hbm, head_bias, order, tgt_hbm,
+    x_hbm, w_hbm, gain_hbm, bias_hbm, mask_hbm, pos_hbm, gains_hbm, head_hbm, hbias_hbm, order_hbm, tgt_hbm,
     g_out, w_out,
     w, pos, head, tgt, lat, lat_in, dlat, dl_all,
-    xb, pack, nq, rstd, acc, d_norm,
+    xb, normed, pack, nq, rstd, d_norm,
     stream, hidden, d_hidden, d_stream, tall, act, act_m, act_v, q, k, v, att, out_b, d_att, back, at, probs, wanted, err, gbuf,
     term, core_x, core_y, d1x, d1y, d2x, d2y, d3x, d3y, d4x, d4y, zr,
     term_e, e1, e2, e3, e4,
+    enc_gain, enc_bias, mask_token, dec_gains, head_bias, order, few_sem,
     w_sem, in_sem, out_sem, lat_send, lat_recv, dl_send, dl_recv, fw_send, fw_recv, nq_send, nq_recv,
     core_send, core_recv, s1, v1, s2, v2, zsend, zrecv,
 ):
@@ -223,51 +224,76 @@
         rows = pl.ds(pl.multiple_of(i * 512, 512), 512)
         return pltpu.make_async_copy(w_hbm.at[rows], w.at[rows], w_sem.at[i])
 
+    few = [(gain_hbm, enc_gain), (bias_hbm, enc_bias), (mask_hbm, mask_token), (gains_hbm, dec_gains)]
+    few += [(hbias_hbm, head_bias), (order_hbm, order)]
+    few = [pltpu.make_async_copy(src, dst, few_sem.at[i]) for i, (src, dst) in enumerate(few)]
     x_copy = pltpu.make_async_copy(x_hbm, xb, in_sem.at[0])
     pos_copy = pltpu.make_async_copy(pos_hbm, pos, in_sem.at[1])
     head_copy = pltpu.make_async_copy(head_hbm, head, in_sem.at[2])
     tgt_copy = pltpu.make_async_copy(tgt_hbm, tgt, in_sem.at[3])
-    lat_copy = remote(lat, lat_in, lat_send.at[0], lat_recv.at[0], to_grp)
+    lat_copies = [remote(lat.at[h], lat_in.at[h], lat_send.at[h], lat_recv.at[h], to_grp) for h in range(2)]
+
+    def w_piece(h, i):
+        part = (pl.ds(i * D, D), pl.ds(h * 512, 512))
+        return pltpu.make_async_copy(w_hbm.at[part], w.at[part], w_sem.at[h * 4 + i])
+
     g_copy = pltpu.make_async_copy(gbuf, g_out, out_sem.at[0])
 
     @pl.when(grp == 0)
     def _():
         x_copy.start()
+        for copy in few[:2]:
+            copy.start()
+        for h in range(2):
+            for i in range(4):
+                w_piece(h, i).start()
 
     @pl.when(grp == 1)
     def _():
+        for copy in few[2:]:
+            copy.start()
         pos_copy.start()
-
-    for i in range(8):
-        w_copy(i).start()
+        for i in range(8):
+            w_copy(i).start()
+
+    def project_half(h):
+        cols = slice(h * 512, (h + 1) * 512)
+        total = jnp.broadcast_to(enc_bias[:, cols], (2 * VIS, 512))
+        for i in range(4):
+            w_piece(h, i).wait()
+            rows = slice(i * D, (i + 1) * D)
+            total = total + nn(normed[:, rows], w[rows, cols])
+        lat[h] = total.astype(B16)
 
     @pl.when(grp == 0)
     def _():
         x_copy.wait()
+        for copy in few[:2]:
+            copy.wait()
         squares = jnp.zeros((2 * VIS, 128), F32)
         for j in range(DE // 128):
             part = xb[:, j * 128 : (j + 1) * 128].astype(F32)
             squares = squares + part * part
         rs = lax.rsqrt(jnp.sum(squares, axis=-1, keepdims=True) * (1.0 / DE) + EPS)
         rstd[...] = jnp.broadcast_to(rs, (2 * VIS, 128))
-        acc[...] = jnp.broadcast_to(enc_bias[...], (2 * VIS, D))
 
         def step(i):
             cols = span(i, 512)
             block = xb[:, cols].astype(F32) * rstd[:, 0:1] * enc_gain[:, cols]
             block = block.astype(B16)
+            normed[:, cols] = block
             for j in range(2):
                 pack[(i % 2) * 2 + j, :, span(i // 2, 256)] = block[:, j * 256 : (j + 1) * 256]
-            w_copy(i).wait()
-            acc[...] += nn(block, w[cols, :])
 
         loop(8, step, 8)
-        lat[...] = acc[...].astype(B16)
+        project_half(0)
 
     @pl.when(grp == 1)
     def _():
         tgt_copy.start()
         head_copy.start()
+        for copy in few[2:]:
+            copy.wait()
         pos_copy.wait()
 
         hi = pos[...].astype(B16)
@@ -304,8 +330,11 @@
 
     @pl.when(grp == 0)
     def _():
-        lat_copy.start()
-        lat_copy.wait_send()
+        lat_copies[0].start()
+        project_half(1)
+        lat_copies[1].start()
+        for copy in lat_copies:
+            copy.wait_send()
         me = z * 2 + c
         nq[me] = pack[me]
         copies = []
@@ -318,11 +347,13 @@
 
     @pl.when(grp == 1)
     def _():
-        lat_copy.wait_recv()
+        for copy in lat_copies:
+            copy.wait_recv()
         gain = dec_gains[0:1, :]
         for s in range(2):
             rows = slice(s * L, s * L + VIS)
-            value = stream[rows, :] + lat_in[s * VIS : (s + 1) * VIS, :].astype(F32)
+            halves = [lat_in[h, s * VIS : (s + 1) * VIS, :] for h in range(2)]
+            value = stream[rows, :] + jnp.concatenate(halves, 1).astype(F32)
             stream[rows, :] = value
             normal = norm_rows(value, gain).astype(B16)
             act[rows, :] = normal
@@ -570,13 +601,13 @@
     grads, w_grad = pl.pallas_call(
         functools.partial(kernel, 1.0 / count),
         out_shape=(jax.ShapeDtypeStruct((2, VIS, DE), B16), jax.ShapeDtypeStruct((64, D), F32)),
-        in_specs=[hbm, hbm, full, full, full, hbm, full, hbm, full, full, hbm],
+        in_specs=[hbm] * 11,
         out_specs=(hbm, full),
         scratch_shapes=[
             V((DE, D), B16), V((L, D), F32), V((D, 256), B16), V((2, L, 256), B16),
-            V((2 * VIS, D), B16), V((2 * VIS, D), B16), V((2 * VIS, D), B16), V((4, 2 * VIS, D), B16),
-            V((2 * VIS, DE), B16), V((4, 2 * VIS, D), B16), V((4, 2 * VIS, D), B16), V((2 * VIS, 128), F32),
-            V((2 * VIS, D), F32), V((2 * VIS, DE), F32),
+            V((2, 2 * VIS, 512), B16), V((2, 2 * VIS, 512), B16), V((2 * VIS, D), B16), V((4, 2 * VIS, D), B16),
+            V((2 * VIS, DE), B16), V((2 * VIS, DE), B16), V((4, 2 * VIS, D), B16), V((4, 2 * VIS, D), B16), V((2 * VIS, 128), F32),
+            V((2 * VIS, DE), F32),
             V((ROWS, D), F32), V((ROWS, D), F32), V((ROWS, D), F32), V((ROWS, D), F32), V((8, ROWS, 128), F32),
             V((ROWS, D), B16), V((ROWS - 2 * VIS, D), B16), V((2 * VIS, D), B16),
             V((ROWS, D), B16), V((ROWS, D), B16), V((ROWS, D), B16), V((ROWS, D), B16),
@@ -591,7 +622,8 @@
             V((4, 2, 4, 32, 256), B16),
             V((2, 4, 4, 64, 512), B16), V((2, 2, 2, 2, 32, 512), B16), V((2, 2, 2, 4, 32, 512), B16),
             V((2, 2, 4, 32, 512), B16), V((2, 2, 3, 32, 512), B16),
-            S((8,)), S((4,)), S((1,)), S((1,)), S((1,)), S((2,)), S((2,)), S((2,)), S((2,)), S((3,)), S((3,)),
+            V((1, DE), F32), V((1, D), F32), V((1, D), F32), V((2, D), F32), V((1, 256), F32), V((2, 1, L), jnp.int32), S((6,)),
+            S((8,)), S((4,)), S((1,)), S((2,)), S((2,)), S((2,)), S((2,)), S((2,)), S((2,)), S((3,)), S((3,)),
             S((4, 2)), S((4, 2)), S((4, 2, 6)), S((4, 2, 6)), S((4, 2, 3)), S((4, 2, 3)), S((4, 2)), S((4, 2)),
         ],
         compiler_params=pltpu.CompilerParams(

time: 66.8 us -> 65 us (0.973); the launches traced: 65.7 us -> 64.8 us
  Pallas kernels: 64.9 us -> 64 us
    pallas_call x1, Pallas kernels: 62.9 us -> 62 us  [on_device(): pl.pallas_call(functools.partial(kernel, 1.0 / count), out_shape=(jax.Sha...]
where the time goes in v5:
time: 65 us; the launch traced here: 64.8 us
  Pallas kernels  64 us (98%)
  between operations  0.84 us (1%)
    pallas_call x1, Pallas kernels, on_device(): pl.pallas_call(functools.partial(kernel, 1.0 / count), out_shape=(jax.Sha...  62 us
    pallas_call x1, Pallas kernels, on_device(): pl.pallas_call(deliver, out_shape=(jax.ShapeDtypeStruct((2, VIS, DE), B16...  1.98 us

profile of v5, /device:TPU:64, one launch (start us, length us, event | category | flops | bytes accessed | tf_op | source)
XLA Modules:
  0.0 64.8 jit_solution(3590487029516678276)
XLA Ops:
  0.6 62.0 %window.1 = (bf16[2,48,4096]{2,1,0:T(8,128)(2,1)}, f32[64,1024]{1,0:T(8,128)}) custom-call(bf16[96,4096]{1,0:T(8,128)(2,1)} %bitcast.12, bf16[4096,1024]{1,0:T(8,128)(2,1)} %bitcast.11, f32[1,4096]{1,0:T(1,128)} %bitcast.14, f32[1,1024]{1,0:T(1,128)} %bitcast.15, f32[1,1024]{1,0:T(1,128)} %bitcast.16, f32[192,1024]{1,0:T(8,128)} %pos_hbm.1, ...), custom_call_target="tpu_custom_call" | custom-call | tf_op jit(solution)/shard_map/window/pallas_call | solution.py:601
  62.7 2.0 %deliver.1 = (bf16[2,48,4096]{2,1,0:T(8,128)(2,1)}, f32[64,1024]{1,0:T(8,128)}) custom-call(bf16[2,48,4096]{2,1,0:T(8,128)(2,1)} %get-tuple-element.6.a_in, f32[64,1024]{1,0:T(8,128)} %get-tuple-element.7.b_in), custom_call_target="tpu_custom_call" | custom-call | tf_op jit(solution)/shard_map/deliver/pallas_call | solution.py:651
